TPU v7x, 256 devices: a whole 4x4x8 slice. The times are simulated.
256 devices in a mesh: dp: 8 (over y, core), fsdp: 32 (over x, z).
Axes of the slice: x: 4, y: 4, z: 8, core: 2. Of those that a mesh axis runs over, the one named last changes fastest.
Arguments:
- kva_parts: bfloat16 [8, 576, 7168], P('dp', 'fsdp'), may hold values from -60 to 60
- kvb_parts: bfloat16 [8, 16384, 512], P('dp', 'fsdp'), may hold values from -60 to 60
- kva_moment: float32 [576, 7168], P('fsdp'), may hold values from -60 to 60
- kvb_moment: float32 [16384, 512], P('fsdp'), may hold values from -60 to 60
Outputs:
- kva_moment_new: float32 [576, 7168], P('fsdp')
- kvb_moment_new: float32 [16384, 512], P('fsdp')
- kva_update: bfloat16 [576, 7168], P('fsdp')
- kvb_update: bfloat16 [16384, 512], P('fsdp')
All inputs are finite; a program needn't handle non-finite values.
Results may differ from a plain program's by a relative error of at most 0.035.
Values may be sent and summed in bfloat16 or wider, within the bound.
No kernel may reach another device: no remote copies, remote signals or barrier semaphores. Data moves between devices by JAX's collectives and lax.ppermute only.
A program may use at most 64 MiB of HBM per device.

v0:
```python
import functools
import math

import jax
import jax.numpy as jnp
from jax import lax
from jax.experimental import pallas as pl
from jax.experimental.pallas import tpu as pltpu
from jax.sharding import Mesh, PartitionSpec as P

D = 7168
KV_RANK = 512
KVA_ROWS = 576
KVB_ROWS = 16384
DP = ("y", "c")
FSDP = ("x", "z")
N_DP = 8
N_FSDP = 32
CHUNK = D // N_DP
GROUPS = CHUNK // 128
MAIN = 16
WIDE = CHUNK + 128
BLOCKS = 5

c1 = 3.4445
c2 = -4.775
c3 = 2.0315
decay_rate = 0.95
norm_epsilon = 1e-07
f32 = jnp.float32
bf16 = jnp.bfloat16
VMEM_LIMIT = 48 * 1024 * 1024
HINT = 40_000_000_000


def call(body, out_shape, n_scalar=0, n_in=1, scratch=(), space=pltpu.VMEM, limit=VMEM_LIMIT, flops=0):
    return pl.pallas_call(
        body,
        out_shape=out_shape,
        in_specs=[pl.BlockSpec(memory_space=pltpu.SMEM)] * n_scalar
        + [pl.BlockSpec(memory_space=space)] * n_in,
        out_specs=jax.tree.map(lambda _: pl.BlockSpec(memory_space=pltpu.VMEM), out_shape),
        scratch_shapes=list(scratch),
        compiler_params=pltpu.CompilerParams(vmem_limit_bytes=limit),
        cost_estimate=pl.CostEstimate(flops=flops, bytes_accessed=0, transcendentals=0)
        if flops
        else None,
    )


def shape(dims, dtype):
    return jax.ShapeDtypeStruct(dims, dtype)


def tail_tile(rows):
    pieces = [rows[:, 128 * k : 128 * k + 128] for k in range(GROUPS)]
    return jnp.concatenate(pieces + [jnp.zeros((2, 128), f32)], axis=0)


def pack_body(c_ref, a_ref, b_ref, o_ref, send_ref, held_ref, sems):
    rows = send_ref.shape[0]
    other = pl.ds(pl.multiple_of((1 - c_ref[0]) * rows, rows), rows)
    copy_a = pltpu.make_async_copy(a_ref, held_ref, sems.at[0])
    copy_b = pltpu.make_async_copy(b_ref.at[0, other], send_ref, sems.at[1])
    copy_a.start()
    copy_b.start()
    copy_a.wait()
    for d in range(N_DP):
        lanes = slice(d * CHUNK, (d + 1) * CHUNK)
        o_ref[d, :, :CHUNK] = held_ref[0, :MAIN, lanes]
        o_ref[d, :, CHUNK:] = tail_tile(held_ref[0, MAIN:, lanes].astype(f32)).astype(bf16)
    copy_b.wait()


def push_a_body(d_ref, parts_ref, m_ref, g_ref, x_ref):
    start = pl.multiple_of(d_ref[0] * CHUNK, 128)
    grad = parts_ref[0].astype(f32)
    for r in range(1, N_DP):
        grad += parts_ref[r].astype(f32)
    g_ref[:MAIN] = grad[:, :KV_RANK].astype(bf16)
    g_ref[MAIN:] = grad[:, KV_RANK:].astype(bf16)
    m_main = m_ref[:MAIN, pl.ds(start, CHUNK)]
    m_tail = tail_tile(m_ref[MAIN:, pl.ds(start, CHUNK)])
    moment = decay_rate * jnp.concatenate([m_main, m_tail], axis=1) + grad
    push = (grad + decay_rate * moment).astype(bf16)
    for r in range(x_ref.shape[0]):
        x_ref[r] = push


def moment_a_body(i_ref, g0_ref, g1_ref, g2_ref, g3_ref, m_ref, o_ref):
    for k, g_ref in enumerate((g0_ref, g1_ref, g2_ref, g3_ref)):
        for c in range(2):
            start = (((i_ref[0] + k) & 3) * 2 + c) * CHUNK
            lanes = pl.ds(pl.multiple_of(start, 128), CHUNK)
            first = KV_RANK // 4 + 2 * MAIN * c
            low = g_ref[first : first + MAIN]
            high = g_ref[first + MAIN : first + 2 * MAIN]
            grad = jnp.concatenate([low, high], axis=1).astype(f32)
            main = grad[:, :CHUNK]
            o_ref[:MAIN, lanes] = decay_rate * m_ref[:MAIN, lanes] + main
            tail = grad[:, CHUNK:]
            for j in range(GROUPS):
                piece = pl.ds(pl.multiple_of(start + 128 * j, 128), 128)
                o_ref[MAIN:, piece] = decay_rate * m_ref[MAIN:, piece] + tail[2 * j : 2 * j + 2]


def half_b_body(c_ref, b_ref, x_ref, o_ref):
    rows = o_ref.shape[0]
    half = b_ref[0, pl.ds(pl.multiple_of(c_ref[0] * rows, rows), rows)]
    o_ref[...] = (half.astype(f32) + x_ref[...].astype(f32)).astype(bf16)


def sum_b_body(b0_ref, b1_ref, b2_ref, b3_ref, g_ref, o_ref):
    rows = b0_ref.shape[0]
    first = b0_ref[...].astype(f32) + b2_ref[...].astype(f32)
    second = b1_ref[...].astype(f32) + b3_ref[...].astype(f32)
    o_ref[:rows] = (first + second).astype(bf16)
    o_ref[rows:] = g_ref[...]


def moment_b_body(d_ref, g_ref, m_ref, o_ref, y_ref, p_ref, a_ref, scratch):
    rows = m_ref.shape[0] // 2
    a_ref[...] = g_ref[:, rows:]
    grad = jnp.concatenate([g_ref[0, :rows], g_ref[1, :rows]], axis=0).astype(f32)
    moment = decay_rate * m_ref[...] + grad
    o_ref[...] = moment
    y = (grad + decay_rate * moment).astype(bf16)
    y_ref[...] = y
    scratch[...] = lax.dot_general(y, y, (((0,), (0,)), ((), ())), preferred_element_type=f32)
    rows = KV_RANK // N_DP
    p_ref[...] = scratch[pl.ds(pl.multiple_of(d_ref[0] * rows, rows), rows), :].astype(bf16)


def gram_a_body(c_ref, x0_ref, x1_ref, x2_ref, x3_ref, own_ref, send_ref, full_ref, gram_ref):
    tails = []
    for k, x_ref in enumerate((x0_ref, x1_ref, x2_ref, x3_ref)):
        full_ref[128 * k : 128 * k + 128] = x_ref[:, :, :CHUNK].reshape(128, CHUNK)
        tails.append(x_ref[:, :, CHUNK:].reshape(128, 128))
    tail = jnp.concatenate(tails, axis=0)
    rows = 2 * N_FSDP
    r = lax.broadcasted_iota(jnp.int32, (rows, N_FSDP * MAIN), 0)
    c = lax.broadcasted_iota(jnp.int32, (rows, N_FSDP * MAIN), 1)
    first = MAIN * lax.shift_right_logical(r, 1) + (r & 1)
    for k in range(GROUPS):
        pick = jnp.where(c == first + 2 * k, 1.0, 0.0).astype(bf16)
        full_ref[N_FSDP * MAIN :, 128 * k : 128 * k + 128] = jnp.dot(
            pick, tail, preferred_element_type=f32
        ).astype(bf16)
    x = full_ref[...]
    gram_ref[...] = jnp.zeros_like(gram_ref)
    gram_ref[:KVA_ROWS, :KVA_ROWS] = lax.dot_general(
        x, x, (((1,), (1,)), ((), ())), preferred_element_type=f32
    )
    for h, o_ref in ((c_ref[0], own_ref), (1 - c_ref[0], send_ref)):
        for i in range(BLOCKS):
            rows = pl.ds(pl.multiple_of(128 * i + 64 * h, 64), 64)
            for j in range(3):
                k = (i + j) % BLOCKS
                o_ref[64 * i : 64 * i + 64, 128 * j : 128 * j + 128] = gram_ref[
                    rows, 128 * k : 128 * k + 128
                ].astype(bf16)


def whole_gram(t_ref, gram_ref):
    for i in range(BLOCKS):
        for j in range(3):
            k = (i + j) % BLOCKS
            block = jnp.concatenate(
                [t_ref[h, 64 * i : 64 * i + 64, 128 * j : 128 * j + 128] for h in range(2)], axis=0
            ).astype(f32)
            gram_ref[128 * i : 128 * i + 128, 128 * k : 128 * k + 128] = block
            if j:
                gram_ref[128 * k : 128 * k + 128, 128 * i : 128 * i + 128] = block.T
    return gram_ref[:KVA_ROWS, :KVA_ROWS]


def mm(a, b):
    return jnp.dot(a.astype(bf16), b.astype(bf16), preferred_element_type=f32)


def symmetric_mm(a, b):
    a, b = a.astype(bf16), b.astype(bf16)
    cut = a.shape[0] // 256 * 256
    if cut == a.shape[0]:
        return jnp.dot(a, b, preferred_element_type=f32)
    left = jnp.dot(a, b[:, :cut], preferred_element_type=f32)
    corner = jnp.dot(a[cut:], b[:, cut:], preferred_element_type=f32)
    right = jnp.concatenate([left[cut:].T, corner], axis=0)
    return jnp.concatenate([left, right], axis=1)


def gram_scale(gram_ref):
    r = lax.broadcasted_iota(jnp.int32, (128, 128), 0)
    c = lax.broadcasted_iota(jnp.int32, (128, 128), 1)
    total = jnp.zeros((128, 128), f32)
    for i in range(gram_ref.shape[0] // 128):
        total += gram_ref[128 * i : 128 * i + 128, 128 * i : 128 * i + 128]
    squares = jnp.sum(jnp.where(r == c, total, 0.0))
    return 1.0 / (jnp.sqrt(squares) + norm_epsilon)


def two_steps(g0):
    d0 = c2 * g0 + c3 * symmetric_mm(g0, g0)
    t0 = c1 * g0 + symmetric_mm(d0, g0)
    g1 = c1 * t0 + symmetric_mm(d0, t0)
    d1 = c2 * g1 + c3 * symmetric_mm(g1, g1)
    d01 = c1 * (d0 + d1) + symmetric_mm(d1, d0)
    t1 = c1 * g1 + symmetric_mm(d1, g1)
    g2 = c1 * t1 + symmetric_mm(d1, t1)
    return d01, g2


def finish_b_body(i_ref, g0_ref, g1_ref, g2_ref, g3_ref, y_ref, o_ref, gram_ref):
    rows = KV_RANK // 4
    for k, g_ref in enumerate((g0_ref, g1_ref, g2_ref, g3_ref)):
        first = pl.multiple_of(((i_ref[0] + k) & 3) * rows, rows)
        gram_ref[pl.ds(first, rows), :] = g_ref[:rows].astype(f32)
    gram = gram_ref[...]
    s = gram_scale(gram_ref)
    d01, g2 = two_steps(gram * (s * s))
    d2 = c2 * g2 + c3 * mm(g2, g2)
    rest = c1 * d01 + c1 * c1 * d2 + mm(d2, d01)
    y = y_ref[...]
    total = s * math.sqrt(max(KVB_ROWS, KV_RANK))
    out = (c1 * c1 * c1) * y.astype(f32) + mm(y, rest)
    o_ref[...] = (out * total).astype(bf16)


def finish_a_body(
    f_ref, c_ref, own_ref, other_ref, x_ref, o_ref, halves_ref, gram_ref, d01_ref, g2_ref
):
    f = f_ref[0]
    halves_ref[c_ref[0]] = own_ref[...]
    halves_ref[1 - c_ref[0]] = other_ref[...]
    gram = whole_gram(halves_ref, gram_ref)
    s = gram_scale(gram_ref)
    d01, g2 = two_steps(gram * (s * s))
    d01_ref[...] = d01
    g2_ref[...] = g2
    main = pl.ds(pl.multiple_of(f * MAIN, MAIN), MAIN)
    base = N_FSDP * MAIN + 8 * lax.shift_right_logical(f, 2)
    tail = pl.ds(pl.multiple_of(base, 8), 8)

    def rows(ref):
        return jnp.concatenate([ref[main, :], ref[tail, :]], axis=0)

    g2_rows = rows(g2_ref)
    d2 = c2 * g2_rows + c3 * mm(g2_rows, g2)
    rest = c1 * rows(d01_ref) + c1 * c1 * d2 + mm(d2, d01)
    x_rows = jnp.concatenate([x_ref[main, :].astype(f32), x_ref[pl.ds(pl.multiple_of(N_FSDP * MAIN + 16 * lax.shift_right_logical(f, 3), 16), 16), :].astype(f32)], axis=0)
    total = s * math.sqrt(max(KVA_ROWS, D))
    moved = mm(rest, x_ref[...])
    out = ((c1 * c1 * c1) * x_rows[:MAIN] + moved[:MAIN]) * total
    o_main = out.astype(bf16)
    q = f & 3
    h = f & 7
    x_tail = x_rows[MAIN : MAIN + 2]
    for j in range(1, 8):
        x_tail = jnp.where(h == j, x_rows[MAIN + 2 * j : MAIN + 2 * j + 2], x_tail)
    m_tail = moved[MAIN : MAIN + 2]
    for j in range(1, 4):
        m_tail = jnp.where(q == j, moved[MAIN + 2 * j : MAIN + 2 * j + 2], m_tail)
    o_tail = tail_tile(((c1 * c1 * c1) * x_tail + m_tail) * total).astype(bf16)
    for r in range(N_DP):
        o_ref[r, :, :CHUNK] = o_main
        o_ref[r, :, CHUNK:] = o_tail


def unpack_body(u_ref, o_ref):
    for d in range(N_DP):
        o_ref[:MAIN, d * CHUNK : (d + 1) * CHUNK] = u_ref[d, :, :CHUNK]
        tail = u_ref[d, :, CHUNK:].astype(f32)
        for k in range(GROUPS):
            piece = slice(d * CHUNK + 128 * k, d * CHUNK + 128 * k + 128)
            o_ref[MAIN:, piece] = tail[2 * k : 2 * k + 2].astype(bf16)


def exchange(x, axis):
    return lax.all_to_all(x, axis, split_axis=0, concat_axis=0, tiled=True)


def total_of(x):
    return jnp.sum(x.astype(f32), axis=0)


def shift(x, axis, n, k):
    return lax.ppermute(x, axis, [(i, (i + k) % n) for i in range(n)])


def others(x, axis, n, step=1):
    return [x] + [shift(x, axis, n, n - k) for k in range(step, n, step)]


def sum_over(x, axis, n, step=1):
    return pair_sums(others(x, axis, n, step))


def pair_sums(terms):
    terms = [y.astype(f32) for y in terms]
    while len(terms) > 1:
        half = len(terms) // 2
        terms = [terms[k] + terms[k + half] for k in range(half)]
    return terms[0].astype(bf16)


def sum_pair(x, axis, n):
    other = lax.ppermute(x, axis, [(i, i ^ 1) for i in range(n)])
    return (x.astype(f32) + other.astype(f32)).astype(bf16)


def local(kva_parts, kvb_parts, kva_moment, kvb_moment):
    y = lax.axis_index("y").astype(jnp.int32).reshape(1)
    c = lax.axis_index("c").astype(jnp.int32).reshape(1)
    z = lax.axis_index("z").astype(jnp.int32).reshape(1)
    d = y * 2 + c
    rows_b = KV_RANK // N_DP

    half = shape((kvb_parts.shape[1] // 2, KV_RANK), bf16)
    packed, send_b = call(
        pack_body,
        (shape((N_DP, MAIN, WIDE), bf16), half),
        1,
        2,
        [pltpu.VMEM(kva_parts.shape, bf16), pltpu.SemaphoreType.DMA((2,))],
        pl.ANY,
        67_000_000,
    )(c, kva_parts, kvb_parts)
    terms_a = exchange(packed, DP)
    grad_b = call(half_b_body, half, 1, 2)(c, kvb_parts, shift(send_b, "c", 2, 1))
    terms_a, grad_b = lax.optimization_barrier((terms_a, grad_b))
    grads_b = others(grad_b, "y", 4)
    grad_a, push_a = call(
        push_a_body,
        (shape((2 * MAIN, KV_RANK), bf16), shape((8, MAIN, WIDE), bf16)),
        1,
        2,
    )(d, terms_a, kva_moment)
    all_z = exchange(push_a, "z")

    rows = half.shape[0]
    both = call(sum_b_body, shape((rows + 2 * MAIN, KV_RANK), bf16), 0, 5, flops=HINT)(
        *grads_b, grad_a
    )
    both = lax.all_gather(both, "c")
    all_z, both = lax.optimization_barrier((all_z, both))
    all_a = others(all_z, "x", 4)
    moment_b, long_b, piece_b, grad_a = call(
        moment_b_body,
        (
            shape(kvb_moment.shape, f32),
            shape(kvb_moment.shape, bf16),
            shape((rows_b, KV_RANK), bf16),
            shape((2, 2 * MAIN, KV_RANK), bf16),
        ),
        1,
        2,
        [pltpu.VMEM((KV_RANK, KV_RANK), f32)],
    )(d, both, kvb_moment)
    terms_b = others(sum_pair(piece_b, "z", 8), "z", 8, 2)

    part = shape((64 * BLOCKS, 384), bf16)
    gram_a, send_a, short_a = call(
        gram_a_body,
        (part, part, shape((KVA_ROWS, CHUNK), bf16)),
        1,
        4,
        [pltpu.VMEM((128 * BLOCKS, 128 * BLOCKS), f32)],
    )(c, *all_a)
    send_a, terms_b = lax.optimization_barrier((send_a, terms_b))
    piece_b = pair_sums(terms_b)
    gram_a = pair_sums([gram_a, shift(send_a, "c", 2, 1)])
    gram_a = sum_over(gram_a, "y", 4)
    piece_b = lax.all_gather(sum_over(piece_b, "x", 4), "c", tiled=True)

    piece_b = jnp.concatenate([piece_b, grad_a.reshape(-1, KV_RANK)])
    gram_a, piece_b = lax.optimization_barrier((gram_a, piece_b))
    other_a = shift(gram_a, "c", 2, 1)
    pieces_b = others(piece_b, "y", 4)
    update_a = call(
        finish_a_body,
        shape((N_DP, MAIN, WIDE), bf16),
        2,
        3,
        [pltpu.VMEM((2,) + part.shape, bf16), pltpu.VMEM((128 * BLOCKS, 128 * BLOCKS), f32)]
        + [pltpu.VMEM((KVA_ROWS, KVA_ROWS), f32)] * 2,
        flops=HINT,
    )(z, c, gram_a, other_a, short_a)
    moment_a = call(moment_a_body, shape(kva_moment.shape, f32), 1, 5)(y, *pieces_b, kva_moment)
    update_a = call(unpack_body, shape(kva_moment.shape, bf16))(exchange(update_a, DP))
    update_b = call(
        finish_b_body,
        shape(long_b.shape, bf16),
        1,
        5,
        [pltpu.VMEM((KV_RANK, KV_RANK), f32)],
        flops=HINT,
    )(y, *pieces_b, long_b)
    return (moment_a, moment_b, update_a, update_b)


def solution(mesh):
    fine = Mesh(mesh.devices.reshape(4, 2, 4, 8), DP + FSDP)
    return jax.shard_map(
        local,
        mesh=fine,
        in_specs=(P(DP, FSDP, None), P(DP, FSDP, None), P(FSDP, None), P(FSDP, None)),
        out_specs=(P(FSDP, None), P(FSDP, None), P(FSDP, None), P(FSDP, None)),
        check_vma=False,
    )
```

profile of v0, /device:TPU:1, one launch (start us, length us, event | category | flops | bytes accessed | tf_op | source)
XLA Modules:
  0.0 97.2 jit_solution(4848188522327401679)
XLA Ops:
  0.6 1.9 %shard_map.75 = (bf16[8,16,1024]{2,1,0:T(8,128)(2,1)}, bf16[256,512]{1,0:T(8,128)(2,1)}) custom-call(s32[1]{0:T(128)} %bitcast.1.c_ref, bf16[1,18,7168]{2,1,0:T(8,128)(2,1)} %a_ref.1, bf16[1,512,512]{2,1,0:T(8,128)(2,1)} %b_ref.3), custom_call_target="tpu_custom_call" | custom-call | tf_op jit(solution)/shard_map/pallas_call | solution.py:319
  2.5 0.0 copy-start.1
  2.5 3.3 %collective-permute-start = (bf16[256,512]{1,0:T(8,128)(2,1)}, bf16[256,512]{1,0:T(8,128)(2,1)S(1)}, u32[]{:S(2)}, u32[]{:S(2)}) collective-permute-start(bf16[256,512]{1,0:T(8,128)(2,1)} %get-tuple-element.27), channel_id=1, source_target_pairs={{0,32},{32,0},{1,33},{33,1},{2,34},{34,2},{3,35},{35,3},{4,36},{36... | collective-permute-start | bytes 786440 | tf_op jit(solution)/shard_map/ppermute | solution.py:287
  5.8 3.5 %all-to-all-start = ((bf16[8,16,1024]{2,1,0:T(8,128)(2,1)}), bf16[8,16,1024]{2,1,0:T(8,128)(2,1)S(1)}, u32[]{:S(2)}, u32[]{:S(2)}) async-start(bf16[8,16,1024]{2,1,0:T(8,128)(2,1)} %get-tuple-element.26), calls=%async_computation | async-start | bytes 524288 | tf_op jit(solution)/shard_map/all_to_all | solution.py:279
  9.3 0.0 collective-permute-done.x_ref
  9.4 0.1 shard_map.76.b0_ref
  9.4 6.4 %all-to-all-done.parts_ref = bf16[8,16,1024]{2,1,0:T(8,128)(2,1)S(1)} async-done(((bf16[8,16,1024]{2,1,0:T(8,128)(2,1)}), bf16[8,16,1024]{2,1,0:T(8,128)(2,1)S(1)}, u32[]{:S(2)}, u32[]{:S(2)}) %all-to-all-start) | async-done | bytes 262176 | tf_op jit(solution)/shard_map/all_to_all | solution.py:279
  15.8 0.3 collective-permute-start.3
  16.1 1.8 %collective-permute-start.2 = (bf16[256,512]{1,0:T(8,128)(2,1)S(1)}, bf16[256,512]{1,0:T(8,128)(2,1)S(1)}, u32[]{:S(2)}, u32[]{:S(2)}) collective-permute-start(bf16[256,512]{1,0:T(8,128)(2,1)S(1)} %shard_map.76.b0_ref), channel_id=1, source_target_pairs={{0,128},{64,192},{128,0},{192,64},{1,129},{65,193},{129,1},{193,65... | collective-permute-start | bytes 786440 | tf_op jit(solution)/shard_map/ppermute | solution.py:287
  17.9 0.6 collective-permute-start.1
  18.5 0.8 shard_map.77
  19.3 7.7 %all-to-all-start.1 = ((bf16[8,16,1024]{2,1,0:T(8,128)(2,1)}), bf16[8,16,1024]{2,1,0:T(8,128)(2,1)S(1)}, u32[]{:S(2)}, u32[]{:S(2)}) async-start(bf16[8,16,1024]{2,1,0:T(8,128)(2,1)} %get-tuple-element.29), calls=%async_computation.1 | async-start | bytes 524288 | tf_op jit(solution)/shard_map/all_to_all | solution.py:279
  27.0 1.9 %collective-permute-done.2.b2_ref = bf16[256,512]{1,0:T(8,128)(2,1)S(1)} collective-permute-done((bf16[256,512]{1,0:T(8,128)(2,1)S(1)}, bf16[256,512]{1,0:T(8,128)(2,1)S(1)}, u32[]{:S(2)}, u32[]{:S(2)}) %collective-permute-start.2) | collective-permute-done | bytes 262176 | tf_op jit(solution)/shard_map/ppermute | solution.py:287
  28.9 1.0 %collective-permute-done.1.b1_ref = bf16[256,512]{1,0:T(8,128)(2,1)S(1)} collective-permute-done((bf16[256,512]{1,0:T(8,128)(2,1)S(1)}, bf16[256,512]{1,0:T(8,128)(2,1)S(1)}, u32[]{:S(2)}, u32[]{:S(2)}) %collective-permute-start.1) | collective-permute-done | bytes 262176 | tf_op jit(solution)/shard_map/ppermute | solution.py:287
  29.8 0.1 shard_map.78
  30.0 4.2 %all-gather = bf16[576,512]{1,0:T(8,128)(2,1)S(1)} all-gather(bf16[288,512]{1,0:T(8,128)(2,1)S(1)} %shard_map.78), channel_id=2, replica_groups=mesh['y'=4,'c'=2,'x'=4,'z'=8] {'c'}, dimensions={0}, use_global_device_ids=true | all-gather | bytes 884736 | tf_op jit(solution)/shard_map/all_gather | solution.py:344
  34.1 2.1 %all-to-all-done.1.x0_ref = bf16[8,16,1024]{2,1,0:T(8,128)(2,1)S(1)} async-done(((bf16[8,16,1024]{2,1,0:T(8,128)(2,1)}), bf16[8,16,1024]{2,1,0:T(8,128)(2,1)S(1)}, u32[]{:S(2)}, u32[]{:S(2)}) %all-to-all-start.1) | async-done | bytes 262176 | tf_op jit(solution)/shard_map/all_to_all | solution.py:279
  36.2 1.2 %shard_map.80 = (f32[512,512]{1,0:T(8,128)}, bf16[512,512]{1,0:T(8,128)(2,1)S(1)}, bf16[64,512]{1,0:T(8,128)(2,1)S(1)}, bf16[2,32,512]{2,1,0:T(8,128)(2,1)S(1)}) custom-call(s32[1]{0:T(128)S(6)} %add.36.d_ref, bf16[2,288,512]{2,1,0:T(8,128)(2,1)S(1)} %bitcast.5, f32[512,512]{1,0:T(8,128)S(1)} %copy-done.2), custom_call_target="tpu_custom_call" | custom-call | tf_op jit(solution)/shard_map/pallas_call | solution.py:347
  37.4 0.1 collective-permute-start.7
  37.5 1.2 %collective-permute-start.6 = (bf16[8,16,1024]{2,1,0:T(8,128)(2,1)S(1)}, bf16[8,16,1024]{2,1,0:T(8,128)(2,1)S(1)}, u32[]{:S(2)}, u32[]{:S(2)}) collective-permute-start(bf16[8,16,1024]{2,1,0:T(8,128)(2,1)S(1)} %all-to-all-done.1.x0_ref), channel_id=1, source_target_pairs={{0,8},{8,16},{16,24},{24,0},{1,9},{9,17},{17,25},{25,1},{2,10},{10... | collective-permute-start | bytes 786440 | tf_op jit(solution)/shard_map/ppermute | solution.py:287
  38.7 2.4 %collective-permute-start.5 = (bf16[8,16,1024]{2,1,0:T(8,128)(2,1)S(1)}, bf16[8,16,1024]{2,1,0:T(8,128)(2,1)S(1)}, u32[]{:S(2)}, u32[]{:S(2)}) collective-permute-start(bf16[8,16,1024]{2,1,0:T(8,128)(2,1)S(1)} %all-to-all-done.1.x0_ref), channel_id=1, source_target_pairs={{0,16},{8,24},{16,0},{24,8},{1,17},{9,25},{17,1},{25,9},{2,18},{10... | collective-permute-start | bytes 786440 | tf_op jit(solution)/shard_map/ppermute | solution.py:287
  41.2 1.2 %collective-permute-start.4 = (bf16[8,16,1024]{2,1,0:T(8,128)(2,1)S(1)}, bf16[8,16,1024]{2,1,0:T(8,128)(2,1)S(1)}, u32[]{:S(2)}, u32[]{:S(2)}) collective-permute-start(bf16[8,16,1024]{2,1,0:T(8,128)(2,1)S(1)} %all-to-all-done.1.x0_ref), channel_id=1, source_target_pairs={{0,24},{8,0},{16,8},{24,16},{1,25},{9,1},{17,9},{25,17},{2,26},{10... | collective-permute-start | bytes 786440 | tf_op jit(solution)/shard_map/ppermute | solution.py:287
  42.3 2.0 %collective-permute-start.10 = (bf16[64,512]{1,0:T(8,128)(2,1)S(1)}, bf16[64,512]{1,0:T(8,128)(2,1)S(1)}, u32[]{:S(2)}, u32[]{:S(2)}) collective-permute-start(bf16[64,512]{1,0:T(8,128)(2,1)S(1)} %add_convert_fusion.4), channel_id=1, source_target_pairs={{0,2},{1,3},{2,4},{3,5},{4,6},{5,7},{6,0},{7,1},{8,10},{9,11},{10,... | collective-permute-start | bytes 196616 | tf_op jit(solution)/shard_map/ppermute | solution.py:287
  44.4 4.2 %collective-permute-start.9 = (bf16[64,512]{1,0:T(8,128)(2,1)S(1)}, bf16[64,512]{1,0:T(8,128)(2,1)S(1)}, u32[]{:S(2)}, u32[]{:S(2)}) collective-permute-start(bf16[64,512]{1,0:T(8,128)(2,1)S(1)} %add_convert_fusion.4), channel_id=1, source_target_pairs={{0,4},{1,5},{2,6},{3,7},{4,0},{5,1},{6,2},{7,3},{8,12},{9,13},{10,... | collective-permute-start | bytes 196616 | tf_op jit(solution)/shard_map/ppermute | solution.py:287
  48.6 2.4 %collective-permute-start.8 = (bf16[64,512]{1,0:T(8,128)(2,1)S(1)}, bf16[64,512]{1,0:T(8,128)(2,1)S(1)}, u32[]{:S(2)}, u32[]{:S(2)}) collective-permute-start(bf16[64,512]{1,0:T(8,128)(2,1)S(1)} %add_convert_fusion.4), channel_id=1, source_target_pairs={{0,6},{1,7},{2,0},{3,1},{4,2},{5,3},{6,4},{7,5},{8,14},{9,15},{10,... | collective-permute-start | bytes 196616 | tf_op jit(solution)/shard_map/ppermute | solution.py:287
  51.0 1.4 %shard_map.79 = (bf16[320,384]{1,0:T(8,128)(2,1)S(1)}, bf16[320,384]{1,0:T(8,128)(2,1)S(1)}, bf16[576,896]{1,0:T(8,128)(2,1)S(1)}) custom-call(s32[1]{0:T(128)} %bitcast.1.c_ref, bf16[8,16,1024]{2,1,0:T(8,128)(2,1)S(1)} %all-to-all-done.1.x0_ref, bf16[8,16,1024]{2,1,0:T(8,128)(2,1)S(1)} %collective-permute-done.4.x1_ref, ...), custom_call_target="tpu_custom_call" | custom-call | tf_op jit(solution)/shard_map/pallas_call | solution.py:362
  52.4 1.2 %collective-permute-done.8 = bf16[64,512]{1,0:T(8,128)(2,1)S(1)} collective-permute-done((bf16[64,512]{1,0:T(8,128)(2,1)S(1)}, bf16[64,512]{1,0:T(8,128)(2,1)S(1)}, u32[]{:S(2)}, u32[]{:S(2)}) %collective-permute-start.8) | collective-permute-done | bytes 65568 | tf_op jit(solution)/shard_map/ppermute | solution.py:287
  53.6 4.9 %collective-permute-start.11 = (bf16[320,384]{1,0:T(8,128)(2,1)S(1)}, bf16[320,384]{1,0:T(8,128)(2,1)S(1)}, u32[]{:S(2)}, u32[]{:S(2)}) collective-permute-start(bf16[320,384]{1,0:T(8,128)(2,1)S(1)} %get-tuple-element.37), channel_id=1, source_target_pairs={{0,32},{32,0},{1,33},{33,1},{2,34},{34,2},{3,35},{35,3},{4,36},{36... | collective-permute-start | bytes 737288 | tf_op jit(solution)/shard_map/ppermute | solution.py:287
  58.5 0.1 collective-permute-start.17
  58.6 2.7 %collective-permute-start.16 = (bf16[64,512]{1,0:T(8,128)(2,1)S(1)}, bf16[64,512]{1,0:T(8,128)(2,1)S(1)}, u32[]{:S(2)}, u32[]{:S(2)}) collective-permute-start(bf16[64,512]{1,0:T(8,128)(2,1)S(1)} %add_convert_fusion.3), channel_id=1, source_target_pairs={{0,24},{8,0},{16,8},{24,16},{1,25},{9,1},{17,9},{25,17},{2,26},{10... | collective-permute-start | bytes 196616 | tf_op jit(solution)/shard_map/ppermute | solution.py:287
  61.3 0.0 collective-permute-start.15
  61.3 0.1 add_convert_fusion.1
  61.4 1.1 %collective-permute-start.14 = (bf16[320,384]{1,0:T(8,128)(2,1)S(1)}, bf16[320,384]{1,0:T(8,128)(2,1)S(1)}, u32[]{:S(2)}, u32[]{:S(2)}) collective-permute-start(bf16[320,384]{1,0:T(8,128)(2,1)S(1)} %add_convert_fusion.1), channel_id=1, source_target_pairs={{0,64},{64,128},{128,192},{192,0},{1,65},{65,129},{129,193},{193,1... | collective-permute-start | bytes 737288 | tf_op jit(solution)/shard_map/ppermute | solution.py:287
  62.5 1.6 %collective-permute-start.13 = (bf16[320,384]{1,0:T(8,128)(2,1)S(1)}, bf16[320,384]{1,0:T(8,128)(2,1)S(1)}, u32[]{:S(2)}, u32[]{:S(2)}) collective-permute-start(bf16[320,384]{1,0:T(8,128)(2,1)S(1)} %add_convert_fusion.1), channel_id=1, source_target_pairs={{0,192},{64,0},{128,64},{192,128},{1,193},{65,1},{129,65},{193,129... | collective-permute-start | bytes 737288 | tf_op jit(solution)/shard_map/ppermute | solution.py:287
  64.1 2.0 %collective-permute-start.12 = (bf16[320,384]{1,0:T(8,128)(2,1)S(1)}, bf16[320,384]{1,0:T(8,128)(2,1)S(1)}, u32[]{:S(2)}, u32[]{:S(2)}) collective-permute-start(bf16[320,384]{1,0:T(8,128)(2,1)S(1)} %add_convert_fusion.1), channel_id=1, source_target_pairs={{0,128},{64,192},{128,0},{192,64},{1,129},{65,193},{129,1},{193,65... | collective-permute-start | bytes 737288 | tf_op jit(solution)/shard_map/ppermute | solution.py:287
  66.2 3.1 %all_gather.11 = bf16[128,512]{1,0:T(8,128)(2,1)S(1)} all-gather(bf16[64,512]{1,0:T(8,128)(2,1)S(1)} %add_convert_fusion.2), channel_id=1, replica_groups=mesh['y'=4,'c'=2,'x'=4,'z'=8] {'c'}, dimensions={0}, use_global_device_ids=true | all-gather | bytes 196608 | tf_op jit(solution)/shard_map/all_gather | solution.py:373
  69.2 0.5 collective-permute-done.14
  69.7 5.1 %collective-permute-done.12 = bf16[320,384]{1,0:T(8,128)(2,1)S(1)} collective-permute-done((bf16[320,384]{1,0:T(8,128)(2,1)S(1)}, bf16[320,384]{1,0:T(8,128)(2,1)S(1)}, u32[]{:S(2)}, u32[]{:S(2)}) %collective-permute-start.12) | collective-permute-done | bytes 245792 | tf_op jit(solution)/shard_map/ppermute | solution.py:287
  74.8 0.1 add_convert_fusion.own_ref
  74.9 1.6 %collective-permute-start.21 = (bf16[320,384]{1,0:T(8,128)(2,1)S(1)}, bf16[320,384]{1,0:T(8,128)(2,1)S(1)}, u32[]{:S(2)}, u32[]{:S(2)}) collective-permute-start(bf16[320,384]{1,0:T(8,128)(2,1)S(1)} %add_convert_fusion.own_ref), channel_id=1, source_target_pairs={{0,32},{32,0},{1,33},{33,1},{2,34},{34,2},{3,35},{35,3},{4,36},{36... | collective-permute-start | bytes 737288 | tf_op jit(solution)/shard_map/ppermute | solution.py:287
  76.5 1.0 %collective-permute-start.20 = (bf16[192,512]{1,0:T(8,128)(2,1)S(1)}, bf16[192,512]{1,0:T(8,128)(2,1)S(1)}, u32[]{:S(2)}, u32[]{:S(2)}) collective-permute-start(bf16[192,512]{1,0:T(8,128)(2,1)S(1)} %pad_maximum_fusion.g0_ref), channel_id=1, source_target_pairs={{0,64},{64,128},{128,192},{192,0},{1,65},{65,129},{129,193},{193,1... | collective-permute-start | bytes 589832 | tf_op jit(solution)/shard_map/ppermute | solution.py:287
  77.6 2.8 %collective-permute-start.19 = (bf16[192,512]{1,0:T(8,128)(2,1)S(1)}, bf16[192,512]{1,0:T(8,128)(2,1)S(1)}, u32[]{:S(2)}, u32[]{:S(2)}) collective-permute-start(bf16[192,512]{1,0:T(8,128)(2,1)S(1)} %pad_maximum_fusion.g0_ref), channel_id=1, source_target_pairs={{0,128},{64,192},{128,0},{192,64},{1,129},{65,193},{129,1},{193,65... | collective-permute-start | bytes 589832 | tf_op jit(solution)/shard_map/ppermute | solution.py:287
  80.4 5.5 %shard_map.82 = bf16[8,16,1024]{2,1,0:T(8,128)(2,1)} custom-call(s32[1]{0:T(128)} %bitcast.4.f_ref, s32[1]{0:T(128)} %bitcast.1.c_ref, bf16[320,384]{1,0:T(8,128)(2,1)S(1)} %add_convert_fusion.own_ref, bf16[320,384]{1,0:T(8,128)(2,1)S(1)} %collective-permute-done.21.other_ref, bf16[576,896]{1,0:T(8,128)(2,1)S(1)} %copy-done.4), custom_call_target="tpu_custom_call" | custom-call | flops 40000000000 | tf_op jit(solution)/shard_map/pallas_call | solution.py:379
  85.9 4.0 %all-to-all-start.2 = ((bf16[8,16,1024]{2,1,0:T(8,128)(2,1)}), bf16[8,16,1024]{2,1,0:T(8,128)(2,1)S(1)}, u32[]{:S(2)}, u32[]{:S(2)}) async-start(bf16[8,16,1024]{2,1,0:T(8,128)(2,1)} %shard_map.82), calls=%async_computation.2 | async-start | bytes 524288 | tf_op jit(solution)/shard_map/all_to_all | solution.py:279
  89.9 4.4 %shard_map.84 = bf16[512,512]{1,0:T(8,128)(2,1)} custom-call(s32[1]{0:T(128)} %bitcast.i_ref, bf16[192,512]{1,0:T(8,128)(2,1)S(1)} %pad_maximum_fusion.g0_ref, bf16[192,512]{1,0:T(8,128)(2,1)S(1)} %collective-permute-done.18.g1_ref, bf16[192,512]{1,0:T(8,128)(2,1)S(1)} %collective-permute-done.19.g2_ref, ...), custom_call_target="tpu_custom_call" | custom-call | flops 40000000000 | tf_op jit(solution)/shard_map/pallas_call | solution.py:390
  94.3 1.0 shard_map.81
  95.3 1.1 %all-to-all-done.2.u_ref = bf16[8,16,1024]{2,1,0:T(8,128)(2,1)S(1)} async-done(((bf16[8,16,1024]{2,1,0:T(8,128)(2,1)}), bf16[8,16,1024]{2,1,0:T(8,128)(2,1)S(1)}, u32[]{:S(2)}, u32[]{:S(2)}) %all-to-all-start.2) | async-done | bytes 262176 | tf_op jit(solution)/shard_map/all_to_all | solution.py:279
  96.4 0.8 shard_map.83
  (30 shorter events, 0.2 us)
Async XLA Ops:
  2.5 6.9 %copy-start.1 = (bf16[1,512,512]{2,1,0:T(8,128)(2,1)S(1)}, bf16[1,512,512]{2,1,0:T(8,128)(2,1)}, u32[]{:S(2)}) copy-start(bf16[1,512,512]{2,1,0:T(8,128)(2,1)} %b_ref.3) | copy-start | bytes 1572868
  2.5 6.8 %collective-permute-start = (bf16[256,512]{1,0:T(8,128)(2,1)}, bf16[256,512]{1,0:T(8,128)(2,1)S(1)}, u32[]{:S(2)}, u32[]{:S(2)}) collective-permute-start(bf16[256,512]{1,0:T(8,128)(2,1)} %get-tuple-element.27), channel_id=1, source_target_pairs={{0,32},{32,0},{1,33},{33,1},{2,34},{34,2},{3,35},{35,3},{4,36},{36... | collective-permute-start | bytes 786440 | tf_op jit(solution)/shard_map/ppermute | solution.py:287
  5.8 12.7 %copy-start = (f32[18,7168]{1,0:T(8,128)S(1)}, f32[18,7168]{1,0:T(8,128)}, u32[]{:S(2)}) copy-start(f32[18,7168]{1,0:T(8,128)} %m_ref.5) | copy-start | bytes 1548292
  5.8 10.0 %all-to-all-start = ((bf16[8,16,1024]{2,1,0:T(8,128)(2,1)}), bf16[8,16,1024]{2,1,0:T(8,128)(2,1)S(1)}, u32[]{:S(2)}, u32[]{:S(2)}) async-start(bf16[8,16,1024]{2,1,0:T(8,128)(2,1)} %get-tuple-element.26), calls=%async_computation | async-start | bytes 524288 | tf_op jit(solution)/shard_map/all_to_all | solution.py:279
  15.8 11.1 %collective-permute-start.3 = (bf16[256,512]{1,0:T(8,128)(2,1)S(1)}, bf16[256,512]{1,0:T(8,128)(2,1)S(1)}, u32[]{:S(2)}, u32[]{:S(2)}) collective-permute-start(bf16[256,512]{1,0:T(8,128)(2,1)S(1)} %shard_map.76.b0_ref), channel_id=1, source_target_pairs={{0,64},{64,128},{128,192},{192,0},{1,65},{65,129},{129,193},{193,1... | collective-permute-start | bytes 786440 | tf_op jit(solution)/shard_map/ppermute | solution.py:287
  16.1 12.7 %collective-permute-start.2 = (bf16[256,512]{1,0:T(8,128)(2,1)S(1)}, bf16[256,512]{1,0:T(8,128)(2,1)S(1)}, u32[]{:S(2)}, u32[]{:S(2)}) collective-permute-start(bf16[256,512]{1,0:T(8,128)(2,1)S(1)} %shard_map.76.b0_ref), channel_id=1, source_target_pairs={{0,128},{64,192},{128,0},{192,64},{1,129},{65,193},{129,1},{193,65... | collective-permute-start | bytes 786440 | tf_op jit(solution)/shard_map/ppermute | solution.py:287
  17.9 11.9 %collective-permute-start.1 = (bf16[256,512]{1,0:T(8,128)(2,1)S(1)}, bf16[256,512]{1,0:T(8,128)(2,1)S(1)}, u32[]{:S(2)}, u32[]{:S(2)}) collective-permute-start(bf16[256,512]{1,0:T(8,128)(2,1)S(1)} %shard_map.76.b0_ref), channel_id=1, source_target_pairs={{0,192},{64,0},{128,64},{192,128},{1,193},{65,1},{129,65},{193,129... | collective-permute-start | bytes 786440 | tf_op jit(solution)/shard_map/ppermute | solution.py:287
  19.3 16.9 %all-to-all-start.1 = ((bf16[8,16,1024]{2,1,0:T(8,128)(2,1)}), bf16[8,16,1024]{2,1,0:T(8,128)(2,1)S(1)}, u32[]{:S(2)}, u32[]{:S(2)}) async-start(bf16[8,16,1024]{2,1,0:T(8,128)(2,1)} %get-tuple-element.29), calls=%async_computation.1 | async-start | bytes 524288 | tf_op jit(solution)/shard_map/all_to_all | solution.py:279
  29.8 6.4 %copy-start.2 = (f32[512,512]{1,0:T(8,128)S(1)}, f32[512,512]{1,0:T(8,128)}, u32[]{:S(2)}) copy-start(f32[512,512]{1,0:T(8,128)} %m_ref.4) | copy-start | bytes 3145732
  37.4 4.9 %collective-permute-start.7 = (bf16[64,512]{1,0:T(8,128)(2,1)S(1)}, bf16[64,512]{1,0:T(8,128)(2,1)S(1)}, u32[]{:S(2)}, u32[]{:S(2)}) collective-permute-start(bf16[64,512]{1,0:T(8,128)(2,1)S(1)} %get-tuple-element.36), channel_id=1, source_target_pairs={{0,1},{1,0},{2,3},{3,2},{4,5},{5,4},{6,7},{7,6},{8,9},{9,8},{10,11... | collective-permute-start | bytes 196616 | tf_op jit(solution)/shard_map/ppermute | solution.py:307
  37.5 11.1 %collective-permute-start.6 = (bf16[8,16,1024]{2,1,0:T(8,128)(2,1)S(1)}, bf16[8,16,1024]{2,1,0:T(8,128)(2,1)S(1)}, u32[]{:S(2)}, u32[]{:S(2)}) collective-permute-start(bf16[8,16,1024]{2,1,0:T(8,128)(2,1)S(1)} %all-to-all-done.1.x0_ref), channel_id=1, source_target_pairs={{0,8},{8,16},{16,24},{24,0},{1,9},{9,17},{17,25},{25,1},{2,10},{10... | collective-permute-start | bytes 786440 | tf_op jit(solution)/shard_map/ppermute | solution.py:287
  38.7 12.3 %collective-permute-start.5 = (bf16[8,16,1024]{2,1,0:T(8,128)(2,1)S(1)}, bf16[8,16,1024]{2,1,0:T(8,128)(2,1)S(1)}, u32[]{:S(2)}, u32[]{:S(2)}) collective-permute-start(bf16[8,16,1024]{2,1,0:T(8,128)(2,1)S(1)} %all-to-all-done.1.x0_ref), channel_id=1, source_target_pairs={{0,16},{8,24},{16,0},{24,8},{1,17},{9,25},{17,1},{25,9},{2,18},{10... | collective-permute-start | bytes 786440 | tf_op jit(solution)/shard_map/ppermute | solution.py:287
  41.2 9.8 %collective-permute-start.4 = (bf16[8,16,1024]{2,1,0:T(8,128)(2,1)S(1)}, bf16[8,16,1024]{2,1,0:T(8,128)(2,1)S(1)}, u32[]{:S(2)}, u32[]{:S(2)}) collective-permute-start(bf16[8,16,1024]{2,1,0:T(8,128)(2,1)S(1)} %all-to-all-done.1.x0_ref), channel_id=1, source_target_pairs={{0,24},{8,0},{16,8},{24,16},{1,25},{9,1},{17,9},{25,17},{2,26},{10... | collective-permute-start | bytes 786440 | tf_op jit(solution)/shard_map/ppermute | solution.py:287
  42.3 10.0 %collective-permute-start.10 = (bf16[64,512]{1,0:T(8,128)(2,1)S(1)}, bf16[64,512]{1,0:T(8,128)(2,1)S(1)}, u32[]{:S(2)}, u32[]{:S(2)}) collective-permute-start(bf16[64,512]{1,0:T(8,128)(2,1)S(1)} %add_convert_fusion.4), channel_id=1, source_target_pairs={{0,2},{1,3},{2,4},{3,5},{4,6},{5,7},{6,0},{7,1},{8,10},{9,11},{10,... | collective-permute-start | bytes 196616 | tf_op jit(solution)/shard_map/ppermute | solution.py:287
  44.4 8.0 %collective-permute-start.9 = (bf16[64,512]{1,0:T(8,128)(2,1)S(1)}, bf16[64,512]{1,0:T(8,128)(2,1)S(1)}, u32[]{:S(2)}, u32[]{:S(2)}) collective-permute-start(bf16[64,512]{1,0:T(8,128)(2,1)S(1)} %add_convert_fusion.4), channel_id=1, source_target_pairs={{0,4},{1,5},{2,6},{3,7},{4,0},{5,1},{6,2},{7,3},{8,12},{9,13},{10,... | collective-permute-start | bytes 196616 | tf_op jit(solution)/shard_map/ppermute | solution.py:287
  48.6 5.0 %collective-permute-start.8 = (bf16[64,512]{1,0:T(8,128)(2,1)S(1)}, bf16[64,512]{1,0:T(8,128)(2,1)S(1)}, u32[]{:S(2)}, u32[]{:S(2)}) collective-permute-start(bf16[64,512]{1,0:T(8,128)(2,1)S(1)} %add_convert_fusion.4), channel_id=1, source_target_pairs={{0,6},{1,7},{2,0},{3,1},{4,2},{5,3},{6,4},{7,5},{8,14},{9,15},{10,... | collective-permute-start | bytes 196616 | tf_op jit(solution)/shard_map/ppermute | solution.py:287
  52.4 16.8 %copy-start.3 = (bf16[576,896]{1,0:T(8,128)(2,1)}, bf16[576,896]{1,0:T(8,128)(2,1)S(1)}, u32[]{:S(2)}) copy-start(bf16[576,896]{1,0:T(8,128)(2,1)S(1)} %get-tuple-element.46.x_ref) | copy-start | bytes 3096580
  53.6 7.7 %collective-permute-start.11 = (bf16[320,384]{1,0:T(8,128)(2,1)S(1)}, bf16[320,384]{1,0:T(8,128)(2,1)S(1)}, u32[]{:S(2)}, u32[]{:S(2)}) collective-permute-start(bf16[320,384]{1,0:T(8,128)(2,1)S(1)} %get-tuple-element.37), channel_id=1, source_target_pairs={{0,32},{32,0},{1,33},{33,1},{2,34},{34,2},{3,35},{35,3},{4,36},{36... | collective-permute-start | bytes 737288 | tf_op jit(solution)/shard_map/ppermute | solution.py:287
  58.5 5.6 %collective-permute-start.17 = (bf16[64,512]{1,0:T(8,128)(2,1)S(1)}, bf16[64,512]{1,0:T(8,128)(2,1)S(1)}, u32[]{:S(2)}, u32[]{:S(2)}) collective-permute-start(bf16[64,512]{1,0:T(8,128)(2,1)S(1)} %add_convert_fusion.3), channel_id=1, source_target_pairs={{0,8},{8,16},{16,24},{24,0},{1,9},{9,17},{17,25},{25,1},{2,10},{10... | collective-permute-start | bytes 196616 | tf_op jit(solution)/shard_map/ppermute | solution.py:287
  58.6 7.5 %collective-permute-start.16 = (bf16[64,512]{1,0:T(8,128)(2,1)S(1)}, bf16[64,512]{1,0:T(8,128)(2,1)S(1)}, u32[]{:S(2)}, u32[]{:S(2)}) collective-permute-start(bf16[64,512]{1,0:T(8,128)(2,1)S(1)} %add_convert_fusion.3), channel_id=1, source_target_pairs={{0,24},{8,0},{16,8},{24,16},{1,25},{9,1},{17,9},{25,17},{2,26},{10... | collective-permute-start | bytes 196616 | tf_op jit(solution)/shard_map/ppermute | solution.py:287
  61.3 4.8 %collective-permute-start.15 = (bf16[64,512]{1,0:T(8,128)(2,1)S(1)}, bf16[64,512]{1,0:T(8,128)(2,1)S(1)}, u32[]{:S(2)}, u32[]{:S(2)}) collective-permute-start(bf16[64,512]{1,0:T(8,128)(2,1)S(1)} %add_convert_fusion.3), channel_id=1, source_target_pairs={{0,16},{8,24},{16,0},{24,8},{1,17},{9,25},{17,1},{25,9},{2,18},{10... | collective-permute-start | bytes 196616 | tf_op jit(solution)/shard_map/ppermute | solution.py:287
  61.4 8.3 %collective-permute-start.14 = (bf16[320,384]{1,0:T(8,128)(2,1)S(1)}, bf16[320,384]{1,0:T(8,128)(2,1)S(1)}, u32[]{:S(2)}, u32[]{:S(2)}) collective-permute-start(bf16[320,384]{1,0:T(8,128)(2,1)S(1)} %add_convert_fusion.1), channel_id=1, source_target_pairs={{0,64},{64,128},{128,192},{192,0},{1,65},{65,129},{129,193},{193,1... | collective-permute-start | bytes 737288 | tf_op jit(solution)/shard_map/ppermute | solution.py:287
  62.5 7.2 %collective-permute-start.13 = (bf16[320,384]{1,0:T(8,128)(2,1)S(1)}, bf16[320,384]{1,0:T(8,128)(2,1)S(1)}, u32[]{:S(2)}, u32[]{:S(2)}) collective-permute-start(bf16[320,384]{1,0:T(8,128)(2,1)S(1)} %add_convert_fusion.1), channel_id=1, source_target_pairs={{0,192},{64,0},{128,64},{192,128},{1,193},{65,1},{129,65},{193,129... | collective-permute-start | bytes 737288 | tf_op jit(solution)/shard_map/ppermute | solution.py:287
  64.1 10.7 %collective-permute-start.12 = (bf16[320,384]{1,0:T(8,128)(2,1)S(1)}, bf16[320,384]{1,0:T(8,128)(2,1)S(1)}, u32[]{:S(2)}, u32[]{:S(2)}) collective-permute-start(bf16[320,384]{1,0:T(8,128)(2,1)S(1)} %add_convert_fusion.1), channel_id=1, source_target_pairs={{0,128},{64,192},{128,0},{192,64},{1,129},{65,193},{129,1},{193,65... | collective-permute-start | bytes 737288 | tf_op jit(solution)/shard_map/ppermute | solution.py:287
  69.2 11.2 %copy-start.4 = (bf16[576,896]{1,0:T(8,128)(2,1)S(1)}, bf16[576,896]{1,0:T(8,128)(2,1)}, u32[]{:S(2)}) copy-start(bf16[576,896]{1,0:T(8,128)(2,1)} %copy-done.3) | copy-start | bytes 3096580
  74.9 5.4 %collective-permute-start.21 = (bf16[320,384]{1,0:T(8,128)(2,1)S(1)}, bf16[320,384]{1,0:T(8,128)(2,1)S(1)}, u32[]{:S(2)}, u32[]{:S(2)}) collective-permute-start(bf16[320,384]{1,0:T(8,128)(2,1)S(1)} %add_convert_fusion.own_ref), channel_id=1, source_target_pairs={{0,32},{32,0},{1,33},{33,1},{2,34},{34,2},{3,35},{35,3},{4,36},{36... | collective-permute-start | bytes 737288 | tf_op jit(solution)/shard_map/ppermute | solution.py:287
  76.5 13.4 %collective-permute-start.20 = (bf16[192,512]{1,0:T(8,128)(2,1)S(1)}, bf16[192,512]{1,0:T(8,128)(2,1)S(1)}, u32[]{:S(2)}, u32[]{:S(2)}) collective-permute-start(bf16[192,512]{1,0:T(8,128)(2,1)S(1)} %pad_maximum_fusion.g0_ref), channel_id=1, source_target_pairs={{0,64},{64,128},{128,192},{192,0},{1,65},{65,129},{129,193},{193,1... | collective-permute-start | bytes 589832 | tf_op jit(solution)/shard_map/ppermute | solution.py:287
  77.6 12.3 %collective-permute-start.19 = (bf16[192,512]{1,0:T(8,128)(2,1)S(1)}, bf16[192,512]{1,0:T(8,128)(2,1)S(1)}, u32[]{:S(2)}, u32[]{:S(2)}) collective-permute-start(bf16[192,512]{1,0:T(8,128)(2,1)S(1)} %pad_maximum_fusion.g0_ref), channel_id=1, source_target_pairs={{0,128},{64,192},{128,0},{192,64},{1,129},{65,193},{129,1},{193,65... | collective-permute-start | bytes 589832 | tf_op jit(solution)/shard_map/ppermute | solution.py:287
  80.4 9.5 %collective-permute-start.18 = (bf16[192,512]{1,0:T(8,128)(2,1)S(1)}, bf16[192,512]{1,0:T(8,128)(2,1)S(1)}, u32[]{:S(2)}, u32[]{:S(2)}) collective-permute-start(bf16[192,512]{1,0:T(8,128)(2,1)S(1)} %pad_maximum_fusion.g0_ref), channel_id=1, source_target_pairs={{0,192},{64,0},{128,64},{192,128},{1,193},{65,1},{129,65},{193,129... | collective-permute-start | bytes 589832 | tf_op jit(solution)/shard_map/ppermute | solution.py:287
  85.9 10.5 %all-to-all-start.2 = ((bf16[8,16,1024]{2,1,0:T(8,128)(2,1)}), bf16[8,16,1024]{2,1,0:T(8,128)(2,1)S(1)}, u32[]{:S(2)}, u32[]{:S(2)}) async-start(bf16[8,16,1024]{2,1,0:T(8,128)(2,1)} %shard_map.82), calls=%async_computation.2 | async-start | bytes 524288 | tf_op jit(solution)/shard_map/all_to_all | solution.py:279
where the time goes:
time: 97.6 us; the launch traced here: 97.2 us
  starting transfers between devices  52.5 us (54%)
  waiting for transfers between devices  19.3 us (20%)
  Pallas kernels  17 us (17%)
  blocking collectives  7.22 us (7%)
    ppermute x21, starting transfers between devices, shift(): return lax.ppermute(x, axis, [(i, (i + k) % n) for i in range(n)])  37.3 us
    all_to_all x3, starting transfers between devices, exchange(): return lax.all_to_all(x, axis, split_axis=0, concat_axis=0, tiled=True)  15.1 us
    ppermute x21, waiting for transfers between devices, shift(): return lax.ppermute(x, axis, [(i, (i + k) % n) for i in range(n)])  9.7 us
    all_to_all x3, waiting for transfers between devices, exchange(): return lax.all_to_all(x, axis, split_axis=0, concat_axis=0, tiled=True)  9.58 us
    pallas_call x1, Pallas kernels, local(): call(finish_a_body, shape((N_DP, MAIN, WIDE), bf16), 2, 3, [pltpu.VMEM((2...  5.52 us
    pallas_call x1, Pallas kernels, local(): call(finish_b_body, shape(long_b.shape, bf16), 1, 5, [pltpu.VMEM((KV_RANK...  4.43 us
    all_gather x1, blocking collectives, local(): both = lax.all_gather(both, 'c')  4.17 us
    all_gather x1, blocking collectives, local(): piece_b = lax.all_gather(sum_over(piece_b, 'x', 4), 'c', tiled=True)  3.05 us
  transfers between devices with their start and end apart: 25, of which 8 were waited for; matrix products, arithmetic and copies ran while one was open for 0% of the time, Pallas kernels for 14%

commit v1 on v0

--- a/solution.py
+++ b/solution.py
@@ -366,7 +366,7 @@
         4,
         [pltpu.VMEM((128 * BLOCKS, 128 * BLOCKS), f32)],
     )(c, *all_a)
-    send_a, terms_b = lax.optimization_barrier((send_a, terms_b))
+    _, terms_b = lax.optimization_barrier((send_a, terms_b))
     piece_b = pair_sums(terms_b)
     gram_a = pair_sums([gram_a, shift(send_a, "c", 2, 1)])
     gram_a = sum_over(gram_a, "y", 4)

time: 97.6 us -> 95.8 us (0.982)
  waiting for transfers between devices: 19.3 us -> 15.1 us
  blocking collectives: 7.22 us -> 9.54 us
    ppermute x21, waiting for transfers between devices: 9.7 us -> 5.52 us  [shift(): return lax.ppermute(x, axis, [(i, (i + k) % n) for i in range(n)])]
    all_gather x1, blocking collectives: 3.05 us -> 5.37 us  [local(): piece_b = lax.all_gather(sum_over(piece_b, 'x', 4), 'c', tiled=True)]
  transfers between devices with their start and end apart: 25 -> 25, of which waited for: 8 -> 6; matrix products, arithmetic and copies ran while one was open for 0% -> 0% of each run, Pallas kernels for 14% -> 14%
where the time goes in v1:
time: 95.8 us; the launch traced here: 95.4 us
  starting transfers between devices  52.6 us (55%)
  Pallas kernels  17 us (18%)
  waiting for transfers between devices  15.1 us (16%)
  blocking collectives  9.54 us (10%)
    ppermute x21, starting transfers between devices, shift(): return lax.ppermute(x, axis, [(i, (i + k) % n) for i in range(n)])  37.4 us
    all_to_all x3, starting transfers between devices, exchange(): return lax.all_to_all(x, axis, split_axis=0, concat_axis=0, tiled=True)  15.1 us
    all_to_all x3, waiting for transfers between devices, exchange(): return lax.all_to_all(x, axis, split_axis=0, concat_axis=0, tiled=True)  9.58 us
    ppermute x21, waiting for transfers between devices, shift(): return lax.ppermute(x, axis, [(i, (i + k) % n) for i in range(n)])  5.52 us
    pallas_call x1, Pallas kernels, local(): call(finish_a_body, shape((N_DP, MAIN, WIDE), bf16), 2, 3, [pltpu.VMEM((2...  5.52 us
    all_gather x1, blocking collectives, local(): piece_b = lax.all_gather(sum_over(piece_b, 'x', 4), 'c', tiled=True)  5.37 us
    pallas_call x1, Pallas kernels, local(): call(finish_b_body, shape(long_b.shape, bf16), 1, 5, [pltpu.VMEM((KV_RANK...  4.43 us
    all_gather x1, blocking collectives, local(): both = lax.all_gather(both, 'c')  4.17 us
  transfers between devices with their start and end apart: 25, of which 6 were waited for; matrix products, arithmetic and copies ran while one was open for 0% of the time, Pallas kernels for 14%

profile of v1, /device:TPU:1, one launch (start us, length us, event | category | flops | bytes accessed | tf_op | source)
XLA Modules:
  0.0 95.4 jit_solution(16216724329164234259)
XLA Ops:
  0.6 1.9 %shard_map.75 = (bf16[8,16,1024]{2,1,0:T(8,128)(2,1)}, bf16[256,512]{1,0:T(8,128)(2,1)}) custom-call(s32[1]{0:T(128)} %bitcast.1.c_ref, bf16[1,18,7168]{2,1,0:T(8,128)(2,1)} %a_ref.1, bf16[1,512,512]{2,1,0:T(8,128)(2,1)} %b_ref.3), custom_call_target="tpu_custom_call" | custom-call | tf_op jit(solution)/shard_map/pallas_call | solution.py:319
  2.5 0.0 copy-start.1
  2.5 3.3 %collective-permute-start = (bf16[256,512]{1,0:T(8,128)(2,1)}, bf16[256,512]{1,0:T(8,128)(2,1)S(1)}, u32[]{:S(2)}, u32[]{:S(2)}) collective-permute-start(bf16[256,512]{1,0:T(8,128)(2,1)} %get-tuple-element.26), channel_id=1, source_target_pairs={{0,32},{32,0},{1,33},{33,1},{2,34},{34,2},{3,35},{35,3},{4,36},{36... | collective-permute-start | bytes 786440 | tf_op jit(solution)/shard_map/ppermute | solution.py:287
  5.8 3.5 %all-to-all-start = ((bf16[8,16,1024]{2,1,0:T(8,128)(2,1)}), bf16[8,16,1024]{2,1,0:T(8,128)(2,1)S(1)}, u32[]{:S(2)}, u32[]{:S(2)}) async-start(bf16[8,16,1024]{2,1,0:T(8,128)(2,1)} %get-tuple-element.25), calls=%async_computation | async-start | bytes 524288 | tf_op jit(solution)/shard_map/all_to_all | solution.py:279
  9.3 0.0 collective-permute-done.x_ref
  9.4 0.1 shard_map.76.b0_ref
  9.4 6.4 %all-to-all-done.parts_ref = bf16[8,16,1024]{2,1,0:T(8,128)(2,1)S(1)} async-done(((bf16[8,16,1024]{2,1,0:T(8,128)(2,1)}), bf16[8,16,1024]{2,1,0:T(8,128)(2,1)S(1)}, u32[]{:S(2)}, u32[]{:S(2)}) %all-to-all-start) | async-done | bytes 262176 | tf_op jit(solution)/shard_map/all_to_all | solution.py:279
  15.8 0.3 collective-permute-start.3
  16.1 1.8 %collective-permute-start.2 = (bf16[256,512]{1,0:T(8,128)(2,1)S(1)}, bf16[256,512]{1,0:T(8,128)(2,1)S(1)}, u32[]{:S(2)}, u32[]{:S(2)}) collective-permute-start(bf16[256,512]{1,0:T(8,128)(2,1)S(1)} %shard_map.76.b0_ref), channel_id=1, source_target_pairs={{0,128},{64,192},{128,0},{192,64},{1,129},{65,193},{129,1},{193,65... | collective-permute-start | bytes 786440 | tf_op jit(solution)/shard_map/ppermute | solution.py:287
  17.9 0.6 collective-permute-start.1
  18.5 0.8 shard_map.77
  19.3 7.7 %all-to-all-start.1 = ((bf16[8,16,1024]{2,1,0:T(8,128)(2,1)}), bf16[8,16,1024]{2,1,0:T(8,128)(2,1)S(1)}, u32[]{:S(2)}, u32[]{:S(2)}) async-start(bf16[8,16,1024]{2,1,0:T(8,128)(2,1)} %get-tuple-element.28), calls=%async_computation.1 | async-start | bytes 524288 | tf_op jit(solution)/shard_map/all_to_all | solution.py:279
  27.0 0.0 collective-permute-done.3.b3_ref
  27.0 1.9 %collective-permute-done.2.b2_ref = bf16[256,512]{1,0:T(8,128)(2,1)S(1)} collective-permute-done((bf16[256,512]{1,0:T(8,128)(2,1)S(1)}, bf16[256,512]{1,0:T(8,128)(2,1)S(1)}, u32[]{:S(2)}, u32[]{:S(2)}) %collective-permute-start.2) | collective-permute-done | bytes 262176 | tf_op jit(solution)/shard_map/ppermute | solution.py:287
  28.9 1.0 %collective-permute-done.1.b1_ref = bf16[256,512]{1,0:T(8,128)(2,1)S(1)} collective-permute-done((bf16[256,512]{1,0:T(8,128)(2,1)S(1)}, bf16[256,512]{1,0:T(8,128)(2,1)S(1)}, u32[]{:S(2)}, u32[]{:S(2)}) %collective-permute-start.1) | collective-permute-done | bytes 262176 | tf_op jit(solution)/shard_map/ppermute | solution.py:287
  29.8 0.1 shard_map.78
  30.0 4.2 %all-gather = bf16[576,512]{1,0:T(8,128)(2,1)S(1)} all-gather(bf16[288,512]{1,0:T(8,128)(2,1)S(1)} %shard_map.78), channel_id=2, replica_groups=mesh['y'=4,'c'=2,'x'=4,'z'=8] {'c'}, dimensions={0}, use_global_device_ids=true | all-gather | bytes 884736 | tf_op jit(solution)/shard_map/all_gather | solution.py:344
  34.1 2.1 %all-to-all-done.1.x0_ref = bf16[8,16,1024]{2,1,0:T(8,128)(2,1)S(1)} async-done(((bf16[8,16,1024]{2,1,0:T(8,128)(2,1)}), bf16[8,16,1024]{2,1,0:T(8,128)(2,1)S(1)}, u32[]{:S(2)}, u32[]{:S(2)}) %all-to-all-start.1) | async-done | bytes 262176 | tf_op jit(solution)/shard_map/all_to_all | solution.py:279
  36.2 1.2 %shard_map.80 = (f32[512,512]{1,0:T(8,128)}, bf16[512,512]{1,0:T(8,128)(2,1)S(1)}, bf16[64,512]{1,0:T(8,128)(2,1)S(1)}, bf16[2,32,512]{2,1,0:T(8,128)(2,1)S(1)}) custom-call(s32[1]{0:T(128)S(6)} %add.36.d_ref, bf16[2,288,512]{2,1,0:T(8,128)(2,1)S(1)} %bitcast.5, f32[512,512]{1,0:T(8,128)S(1)} %copy-done.2), custom_call_target="tpu_custom_call" | custom-call | tf_op jit(solution)/shard_map/pallas_call | solution.py:347
  37.4 0.1 collective-permute-start.11
  37.5 1.2 %collective-permute-start.6 = (bf16[8,16,1024]{2,1,0:T(8,128)(2,1)S(1)}, bf16[8,16,1024]{2,1,0:T(8,128)(2,1)S(1)}, u32[]{:S(2)}, u32[]{:S(2)}) collective-permute-start(bf16[8,16,1024]{2,1,0:T(8,128)(2,1)S(1)} %all-to-all-done.1.x0_ref), channel_id=1, source_target_pairs={{0,8},{8,16},{16,24},{24,0},{1,9},{9,17},{17,25},{25,1},{2,10},{10... | collective-permute-start | bytes 786440 | tf_op jit(solution)/shard_map/ppermute | solution.py:287
  38.7 2.4 %collective-permute-start.5 = (bf16[8,16,1024]{2,1,0:T(8,128)(2,1)S(1)}, bf16[8,16,1024]{2,1,0:T(8,128)(2,1)S(1)}, u32[]{:S(2)}, u32[]{:S(2)}) collective-permute-start(bf16[8,16,1024]{2,1,0:T(8,128)(2,1)S(1)} %all-to-all-done.1.x0_ref), channel_id=1, source_target_pairs={{0,16},{8,24},{16,0},{24,8},{1,17},{9,25},{17,1},{25,9},{2,18},{10... | collective-permute-start | bytes 786440 | tf_op jit(solution)/shard_map/ppermute | solution.py:287
  41.2 1.2 %collective-permute-start.4 = (bf16[8,16,1024]{2,1,0:T(8,128)(2,1)S(1)}, bf16[8,16,1024]{2,1,0:T(8,128)(2,1)S(1)}, u32[]{:S(2)}, u32[]{:S(2)}) collective-permute-start(bf16[8,16,1024]{2,1,0:T(8,128)(2,1)S(1)} %all-to-all-done.1.x0_ref), channel_id=1, source_target_pairs={{0,24},{8,0},{16,8},{24,16},{1,25},{9,1},{17,9},{25,17},{2,26},{10... | collective-permute-start | bytes 786440 | tf_op jit(solution)/shard_map/ppermute | solution.py:287
  42.3 2.0 %collective-permute-start.14 = (bf16[64,512]{1,0:T(8,128)(2,1)S(1)}, bf16[64,512]{1,0:T(8,128)(2,1)S(1)}, u32[]{:S(2)}, u32[]{:S(2)}) collective-permute-start(bf16[64,512]{1,0:T(8,128)(2,1)S(1)} %add_convert_fusion.4), channel_id=1, source_target_pairs={{0,2},{1,3},{2,4},{3,5},{4,6},{5,7},{6,0},{7,1},{8,10},{9,11},{10,... | collective-permute-start | bytes 196616 | tf_op jit(solution)/shard_map/ppermute | solution.py:287
  44.4 4.2 %collective-permute-start.13 = (bf16[64,512]{1,0:T(8,128)(2,1)S(1)}, bf16[64,512]{1,0:T(8,128)(2,1)S(1)}, u32[]{:S(2)}, u32[]{:S(2)}) collective-permute-start(bf16[64,512]{1,0:T(8,128)(2,1)S(1)} %add_convert_fusion.4), channel_id=1, source_target_pairs={{0,4},{1,5},{2,6},{3,7},{4,0},{5,1},{6,2},{7,3},{8,12},{9,13},{10,... | collective-permute-start | bytes 196616 | tf_op jit(solution)/shard_map/ppermute | solution.py:287
  48.6 0.0 collective-permute-done.6.x3_ref
  48.6 2.4 %collective-permute-start.12 = (bf16[64,512]{1,0:T(8,128)(2,1)S(1)}, bf16[64,512]{1,0:T(8,128)(2,1)S(1)}, u32[]{:S(2)}, u32[]{:S(2)}) collective-permute-start(bf16[64,512]{1,0:T(8,128)(2,1)S(1)} %add_convert_fusion.4), channel_id=1, source_target_pairs={{0,6},{1,7},{2,0},{3,1},{4,2},{5,3},{6,4},{7,5},{8,14},{9,15},{10,... | collective-permute-start | bytes 196616 | tf_op jit(solution)/shard_map/ppermute | solution.py:287
  51.0 1.4 %shard_map.79 = (bf16[320,384]{1,0:T(8,128)(2,1)S(1)}, bf16[320,384]{1,0:T(8,128)(2,1)S(1)}, bf16[576,896]{1,0:T(8,128)(2,1)S(1)}) custom-call(s32[1]{0:T(128)} %bitcast.1.c_ref, bf16[8,16,1024]{2,1,0:T(8,128)(2,1)S(1)} %all-to-all-done.1.x0_ref, bf16[8,16,1024]{2,1,0:T(8,128)(2,1)S(1)} %collective-permute-done.4.x1_ref, ...), custom_call_target="tpu_custom_call" | custom-call | tf_op jit(solution)/shard_map/pallas_call | solution.py:362
  52.4 3.1 %collective-permute-start.7 = (bf16[320,384]{1,0:T(8,128)(2,1)S(1)}, bf16[320,384]{1,0:T(8,128)(2,1)S(1)}, u32[]{:S(2)}, u32[]{:S(2)}) collective-permute-start(bf16[320,384]{1,0:T(8,128)(2,1)S(1)} %get-tuple-element.33), channel_id=1, source_target_pairs={{0,32},{32,0},{1,33},{33,1},{2,34},{34,2},{3,35},{35,3},{4,36},{36... | collective-permute-start | bytes 737288 | tf_op jit(solution)/shard_map/ppermute | solution.py:287
  55.6 1.1 %collective-permute-start.17 = (bf16[64,512]{1,0:T(8,128)(2,1)S(1)}, bf16[64,512]{1,0:T(8,128)(2,1)S(1)}, u32[]{:S(2)}, u32[]{:S(2)}) collective-permute-start(bf16[64,512]{1,0:T(8,128)(2,1)S(1)} %add_convert_fusion.3), channel_id=1, source_target_pairs={{0,8},{8,16},{16,24},{24,0},{1,9},{9,17},{17,25},{25,1},{2,10},{10... | collective-permute-start | bytes 196616 | tf_op jit(solution)/shard_map/ppermute | solution.py:287
  56.7 1.6 %collective-permute-start.16 = (bf16[64,512]{1,0:T(8,128)(2,1)S(1)}, bf16[64,512]{1,0:T(8,128)(2,1)S(1)}, u32[]{:S(2)}, u32[]{:S(2)}) collective-permute-start(bf16[64,512]{1,0:T(8,128)(2,1)S(1)} %add_convert_fusion.3), channel_id=1, source_target_pairs={{0,24},{8,0},{16,8},{24,16},{1,25},{9,1},{17,9},{25,17},{2,26},{10... | collective-permute-start | bytes 196616 | tf_op jit(solution)/shard_map/ppermute | solution.py:287
  58.3 1.2 %collective-permute-start.15 = (bf16[64,512]{1,0:T(8,128)(2,1)S(1)}, bf16[64,512]{1,0:T(8,128)(2,1)S(1)}, u32[]{:S(2)}, u32[]{:S(2)}) collective-permute-start(bf16[64,512]{1,0:T(8,128)(2,1)S(1)} %add_convert_fusion.3), channel_id=1, source_target_pairs={{0,16},{8,24},{16,0},{24,8},{1,17},{9,25},{17,1},{25,9},{2,18},{10... | collective-permute-start | bytes 196616 | tf_op jit(solution)/shard_map/ppermute | solution.py:287
  59.5 0.1 add_convert_fusion.1
  59.6 1.2 %collective-permute-start.10 = (bf16[320,384]{1,0:T(8,128)(2,1)S(1)}, bf16[320,384]{1,0:T(8,128)(2,1)S(1)}, u32[]{:S(2)}, u32[]{:S(2)}) collective-permute-start(bf16[320,384]{1,0:T(8,128)(2,1)S(1)} %add_convert_fusion.1), channel_id=1, source_target_pairs={{0,64},{64,128},{128,192},{192,0},{1,65},{65,129},{129,193},{193,1... | collective-permute-start | bytes 737288 | tf_op jit(solution)/shard_map/ppermute | solution.py:287
  60.8 1.5 %collective-permute-start.9 = (bf16[320,384]{1,0:T(8,128)(2,1)S(1)}, bf16[320,384]{1,0:T(8,128)(2,1)S(1)}, u32[]{:S(2)}, u32[]{:S(2)}) collective-permute-start(bf16[320,384]{1,0:T(8,128)(2,1)S(1)} %add_convert_fusion.1), channel_id=1, source_target_pairs={{0,192},{64,0},{128,64},{192,128},{1,193},{65,1},{129,65},{193,129... | collective-permute-start | bytes 737288 | tf_op jit(solution)/shard_map/ppermute | solution.py:287
  62.4 1.4 %collective-permute-start.8 = (bf16[320,384]{1,0:T(8,128)(2,1)S(1)}, bf16[320,384]{1,0:T(8,128)(2,1)S(1)}, u32[]{:S(2)}, u32[]{:S(2)}) collective-permute-start(bf16[320,384]{1,0:T(8,128)(2,1)S(1)} %add_convert_fusion.1), channel_id=1, source_target_pairs={{0,128},{64,192},{128,0},{192,64},{1,129},{65,193},{129,1},{193,65... | collective-permute-start | bytes 737288 | tf_op jit(solution)/shard_map/ppermute | solution.py:287
  63.8 5.4 %all_gather.11 = bf16[128,512]{1,0:T(8,128)(2,1)S(1)} all-gather(bf16[64,512]{1,0:T(8,128)(2,1)S(1)} %add_convert_fusion.2), channel_id=1, replica_groups=mesh['y'=4,'c'=2,'x'=4,'z'=8] {'c'}, dimensions={0}, use_global_device_ids=true | all-gather | bytes 196608 | tf_op jit(solution)/shard_map/all_gather | solution.py:373
  69.2 2.6 %collective-permute-done.8 = bf16[320,384]{1,0:T(8,128)(2,1)S(1)} collective-permute-done((bf16[320,384]{1,0:T(8,128)(2,1)S(1)}, bf16[320,384]{1,0:T(8,128)(2,1)S(1)}, u32[]{:S(2)}, u32[]{:S(2)}) %collective-permute-start.8) | collective-permute-done | bytes 245792 | tf_op jit(solution)/shard_map/ppermute | solution.py:287
  71.8 0.1 add_convert_fusion.own_ref
  72.0 2.9 %collective-permute-start.21 = (bf16[320,384]{1,0:T(8,128)(2,1)S(1)}, bf16[320,384]{1,0:T(8,128)(2,1)S(1)}, u32[]{:S(2)}, u32[]{:S(2)}) collective-permute-start(bf16[320,384]{1,0:T(8,128)(2,1)S(1)} %add_convert_fusion.own_ref), channel_id=1, source_target_pairs={{0,32},{32,0},{1,33},{33,1},{2,34},{34,2},{3,35},{35,3},{4,36},{36... | collective-permute-start | bytes 737288 | tf_op jit(solution)/shard_map/ppermute | solution.py:287
  74.9 1.0 %collective-permute-start.20 = (bf16[192,512]{1,0:T(8,128)(2,1)S(1)}, bf16[192,512]{1,0:T(8,128)(2,1)S(1)}, u32[]{:S(2)}, u32[]{:S(2)}) collective-permute-start(bf16[192,512]{1,0:T(8,128)(2,1)S(1)} %pad_maximum_fusion.g0_ref), channel_id=1, source_target_pairs={{0,64},{64,128},{128,192},{192,0},{1,65},{65,129},{129,193},{193,1... | collective-permute-start | bytes 589832 | tf_op jit(solution)/shard_map/ppermute | solution.py:287
  75.9 2.8 %collective-permute-start.19 = (bf16[192,512]{1,0:T(8,128)(2,1)S(1)}, bf16[192,512]{1,0:T(8,128)(2,1)S(1)}, u32[]{:S(2)}, u32[]{:S(2)}) collective-permute-start(bf16[192,512]{1,0:T(8,128)(2,1)S(1)} %pad_maximum_fusion.g0_ref), channel_id=1, source_target_pairs={{0,128},{64,192},{128,0},{192,64},{1,129},{65,193},{129,1},{193,65... | collective-permute-start | bytes 589832 | tf_op jit(solution)/shard_map/ppermute | solution.py:287
  78.6 5.5 %shard_map.82 = bf16[8,16,1024]{2,1,0:T(8,128)(2,1)} custom-call(s32[1]{0:T(128)} %bitcast.4.f_ref, s32[1]{0:T(128)} %bitcast.1.c_ref, bf16[320,384]{1,0:T(8,128)(2,1)S(1)} %add_convert_fusion.own_ref, bf16[320,384]{1,0:T(8,128)(2,1)S(1)} %collective-permute-done.21.other_ref, bf16[576,896]{1,0:T(8,128)(2,1)S(1)} %copy-done.4), custom_call_target="tpu_custom_call" | custom-call | flops 40000000000 | tf_op jit(solution)/shard_map/pallas_call | solution.py:379
  84.1 4.0 %all-to-all-start.2 = ((bf16[8,16,1024]{2,1,0:T(8,128)(2,1)}), bf16[8,16,1024]{2,1,0:T(8,128)(2,1)S(1)}, u32[]{:S(2)}, u32[]{:S(2)}) async-start(bf16[8,16,1024]{2,1,0:T(8,128)(2,1)} %shard_map.82), calls=%async_computation.2 | async-start | bytes 524288 | tf_op jit(solution)/shard_map/all_to_all | solution.py:279
  88.1 4.4 %shard_map.84 = bf16[512,512]{1,0:T(8,128)(2,1)} custom-call(s32[1]{0:T(128)} %bitcast.i_ref, bf16[192,512]{1,0:T(8,128)(2,1)S(1)} %pad_maximum_fusion.g0_ref, bf16[192,512]{1,0:T(8,128)(2,1)S(1)} %collective-permute-done.18.g1_ref, bf16[192,512]{1,0:T(8,128)(2,1)S(1)} %collective-permute-done.19.g2_ref, ...), custom_call_target="tpu_custom_call" | custom-call | flops 40000000000 | tf_op jit(solution)/shard_map/pallas_call | solution.py:390
  92.5 1.0 %shard_map.81 = f32[18,7168]{1,0:T(8,128)} custom-call(s32[1]{0:T(128)} %bitcast.i_ref, bf16[192,512]{1,0:T(8,128)(2,1)S(1)} %pad_maximum_fusion.g0_ref, bf16[192,512]{1,0:T(8,128)(2,1)S(1)} %collective-permute-done.18.g1_ref, bf16[192,512]{1,0:T(8,128)(2,1)S(1)} %collective-permute-done.19.g2_ref, bf16[192,512]{1,0:T(8,128)(2,1)S(1)} %collective-permute-done.20.g3_ref, ...), custom_call_target="tpu_custom_call" | custom-call | tf_op jit(solution)/shard_map/pallas_call | solution.py:388
  93.5 1.1 %all-to-all-done.2.u_ref = bf16[8,16,1024]{2,1,0:T(8,128)(2,1)S(1)} async-done(((bf16[8,16,1024]{2,1,0:T(8,128)(2,1)}), bf16[8,16,1024]{2,1,0:T(8,128)(2,1)S(1)}, u32[]{:S(2)}, u32[]{:S(2)}) %all-to-all-start.2) | async-done | bytes 262176 | tf_op jit(solution)/shard_map/all_to_all | solution.py:279
  94.6 0.8 shard_map.83
  (30 shorter events, 0.2 us)
Async XLA Ops:
  2.5 6.9 %copy-start.1 = (bf16[1,512,512]{2,1,0:T(8,128)(2,1)S(1)}, bf16[1,512,512]{2,1,0:T(8,128)(2,1)}, u32[]{:S(2)}) copy-start(bf16[1,512,512]{2,1,0:T(8,128)(2,1)} %b_ref.3) | copy-start | bytes 1572868
  2.5 6.8 %collective-permute-start = (bf16[256,512]{1,0:T(8,128)(2,1)}, bf16[256,512]{1,0:T(8,128)(2,1)S(1)}, u32[]{:S(2)}, u32[]{:S(2)}) collective-permute-start(bf16[256,512]{1,0:T(8,128)(2,1)} %get-tuple-element.26), channel_id=1, source_target_pairs={{0,32},{32,0},{1,33},{33,1},{2,34},{34,2},{3,35},{35,3},{4,36},{36... | collective-permute-start | bytes 786440 | tf_op jit(solution)/shard_map/ppermute | solution.py:287
  5.8 12.7 %copy-start = (f32[18,7168]{1,0:T(8,128)S(1)}, f32[18,7168]{1,0:T(8,128)}, u32[]{:S(2)}) copy-start(f32[18,7168]{1,0:T(8,128)} %m_ref.5) | copy-start | bytes 1548292
  5.8 10.0 %all-to-all-start = ((bf16[8,16,1024]{2,1,0:T(8,128)(2,1)}), bf16[8,16,1024]{2,1,0:T(8,128)(2,1)S(1)}, u32[]{:S(2)}, u32[]{:S(2)}) async-start(bf16[8,16,1024]{2,1,0:T(8,128)(2,1)} %get-tuple-element.25), calls=%async_computation | async-start | bytes 524288 | tf_op jit(solution)/shard_map/all_to_all | solution.py:279
  15.8 11.1 %collective-permute-start.3 = (bf16[256,512]{1,0:T(8,128)(2,1)S(1)}, bf16[256,512]{1,0:T(8,128)(2,1)S(1)}, u32[]{:S(2)}, u32[]{:S(2)}) collective-permute-start(bf16[256,512]{1,0:T(8,128)(2,1)S(1)} %shard_map.76.b0_ref), channel_id=1, source_target_pairs={{0,64},{64,128},{128,192},{192,0},{1,65},{65,129},{129,193},{193,1... | collective-permute-start | bytes 786440 | tf_op jit(solution)/shard_map/ppermute | solution.py:287
  16.1 12.7 %collective-permute-start.2 = (bf16[256,512]{1,0:T(8,128)(2,1)S(1)}, bf16[256,512]{1,0:T(8,128)(2,1)S(1)}, u32[]{:S(2)}, u32[]{:S(2)}) collective-permute-start(bf16[256,512]{1,0:T(8,128)(2,1)S(1)} %shard_map.76.b0_ref), channel_id=1, source_target_pairs={{0,128},{64,192},{128,0},{192,64},{1,129},{65,193},{129,1},{193,65... | collective-permute-start | bytes 786440 | tf_op jit(solution)/shard_map/ppermute | solution.py:287
  17.9 11.9 %collective-permute-start.1 = (bf16[256,512]{1,0:T(8,128)(2,1)S(1)}, bf16[256,512]{1,0:T(8,128)(2,1)S(1)}, u32[]{:S(2)}, u32[]{:S(2)}) collective-permute-start(bf16[256,512]{1,0:T(8,128)(2,1)S(1)} %shard_map.76.b0_ref), channel_id=1, source_target_pairs={{0,192},{64,0},{128,64},{192,128},{1,193},{65,1},{129,65},{193,129... | collective-permute-start | bytes 786440 | tf_op jit(solution)/shard_map/ppermute | solution.py:287
  19.3 16.9 %all-to-all-start.1 = ((bf16[8,16,1024]{2,1,0:T(8,128)(2,1)}), bf16[8,16,1024]{2,1,0:T(8,128)(2,1)S(1)}, u32[]{:S(2)}, u32[]{:S(2)}) async-start(bf16[8,16,1024]{2,1,0:T(8,128)(2,1)} %get-tuple-element.28), calls=%async_computation.1 | async-start | bytes 524288 | tf_op jit(solution)/shard_map/all_to_all | solution.py:279
  29.8 6.4 %copy-start.2 = (f32[512,512]{1,0:T(8,128)S(1)}, f32[512,512]{1,0:T(8,128)}, u32[]{:S(2)}) copy-start(f32[512,512]{1,0:T(8,128)} %m_ref.4) | copy-start | bytes 3145732
  37.4 4.9 %collective-permute-start.11 = (bf16[64,512]{1,0:T(8,128)(2,1)S(1)}, bf16[64,512]{1,0:T(8,128)(2,1)S(1)}, u32[]{:S(2)}, u32[]{:S(2)}) collective-permute-start(bf16[64,512]{1,0:T(8,128)(2,1)S(1)} %get-tuple-element.35), channel_id=1, source_target_pairs={{0,1},{1,0},{2,3},{3,2},{4,5},{5,4},{6,7},{7,6},{8,9},{9,8},{10,11... | collective-permute-start | bytes 196616 | tf_op jit(solution)/shard_map/ppermute | solution.py:307
  37.5 11.1 %collective-permute-start.6 = (bf16[8,16,1024]{2,1,0:T(8,128)(2,1)S(1)}, bf16[8,16,1024]{2,1,0:T(8,128)(2,1)S(1)}, u32[]{:S(2)}, u32[]{:S(2)}) collective-permute-start(bf16[8,16,1024]{2,1,0:T(8,128)(2,1)S(1)} %all-to-all-done.1.x0_ref), channel_id=1, source_target_pairs={{0,8},{8,16},{16,24},{24,0},{1,9},{9,17},{17,25},{25,1},{2,10},{10... | collective-permute-start | bytes 786440 | tf_op jit(solution)/shard_map/ppermute | solution.py:287
  38.7 12.3 %collective-permute-start.5 = (bf16[8,16,1024]{2,1,0:T(8,128)(2,1)S(1)}, bf16[8,16,1024]{2,1,0:T(8,128)(2,1)S(1)}, u32[]{:S(2)}, u32[]{:S(2)}) collective-permute-start(bf16[8,16,1024]{2,1,0:T(8,128)(2,1)S(1)} %all-to-all-done.1.x0_ref), channel_id=1, source_target_pairs={{0,16},{8,24},{16,0},{24,8},{1,17},{9,25},{17,1},{25,9},{2,18},{10... | collective-permute-start | bytes 786440 | tf_op jit(solution)/shard_map/ppermute | solution.py:287
  41.2 9.8 %collective-permute-start.4 = (bf16[8,16,1024]{2,1,0:T(8,128)(2,1)S(1)}, bf16[8,16,1024]{2,1,0:T(8,128)(2,1)S(1)}, u32[]{:S(2)}, u32[]{:S(2)}) collective-permute-start(bf16[8,16,1024]{2,1,0:T(8,128)(2,1)S(1)} %all-to-all-done.1.x0_ref), channel_id=1, source_target_pairs={{0,24},{8,0},{16,8},{24,16},{1,25},{9,1},{17,9},{25,17},{2,26},{10... | collective-permute-start | bytes 786440 | tf_op jit(solution)/shard_map/ppermute | solution.py:287
  42.3 13.2 %collective-permute-start.14 = (bf16[64,512]{1,0:T(8,128)(2,1)S(1)}, bf16[64,512]{1,0:T(8,128)(2,1)S(1)}, u32[]{:S(2)}, u32[]{:S(2)}) collective-permute-start(bf16[64,512]{1,0:T(8,128)(2,1)S(1)} %add_convert_fusion.4), channel_id=1, source_target_pairs={{0,2},{1,3},{2,4},{3,5},{4,6},{5,7},{6,0},{7,1},{8,10},{9,11},{10,... | collective-permute-start | bytes 196616 | tf_op jit(solution)/shard_map/ppermute | solution.py:287
  44.4 11.1 %collective-permute-start.13 = (bf16[64,512]{1,0:T(8,128)(2,1)S(1)}, bf16[64,512]{1,0:T(8,128)(2,1)S(1)}, u32[]{:S(2)}, u32[]{:S(2)}) collective-permute-start(bf16[64,512]{1,0:T(8,128)(2,1)S(1)} %add_convert_fusion.4), channel_id=1, source_target_pairs={{0,4},{1,5},{2,6},{3,7},{4,0},{5,1},{6,2},{7,3},{8,12},{9,13},{10,... | collective-permute-start | bytes 196616 | tf_op jit(solution)/shard_map/ppermute | solution.py:287
  48.6 6.9 %collective-permute-start.12 = (bf16[64,512]{1,0:T(8,128)(2,1)S(1)}, bf16[64,512]{1,0:T(8,128)(2,1)S(1)}, u32[]{:S(2)}, u32[]{:S(2)}) collective-permute-start(bf16[64,512]{1,0:T(8,128)(2,1)S(1)} %add_convert_fusion.4), channel_id=1, source_target_pairs={{0,6},{1,7},{2,0},{3,1},{4,2},{5,3},{6,4},{7,5},{8,14},{9,15},{10,... | collective-permute-start | bytes 196616 | tf_op jit(solution)/shard_map/ppermute | solution.py:287
  52.4 16.8 %copy-start.3 = (bf16[576,896]{1,0:T(8,128)(2,1)}, bf16[576,896]{1,0:T(8,128)(2,1)S(1)}, u32[]{:S(2)}) copy-start(bf16[576,896]{1,0:T(8,128)(2,1)S(1)} %get-tuple-element.44.x_ref) | copy-start | bytes 3096580
  52.4 7.2 %collective-permute-start.7 = (bf16[320,384]{1,0:T(8,128)(2,1)S(1)}, bf16[320,384]{1,0:T(8,128)(2,1)S(1)}, u32[]{:S(2)}, u32[]{:S(2)}) collective-permute-start(bf16[320,384]{1,0:T(8,128)(2,1)S(1)} %get-tuple-element.33), channel_id=1, source_target_pairs={{0,32},{32,0},{1,33},{33,1},{2,34},{34,2},{3,35},{35,3},{4,36},{36... | collective-permute-start | bytes 737288 | tf_op jit(solution)/shard_map/ppermute | solution.py:287
  55.6 6.8 %collective-permute-start.17 = (bf16[64,512]{1,0:T(8,128)(2,1)S(1)}, bf16[64,512]{1,0:T(8,128)(2,1)S(1)}, u32[]{:S(2)}, u32[]{:S(2)}) collective-permute-start(bf16[64,512]{1,0:T(8,128)(2,1)S(1)} %add_convert_fusion.3), channel_id=1, source_target_pairs={{0,8},{8,16},{16,24},{24,0},{1,9},{9,17},{17,25},{25,1},{2,10},{10... | collective-permute-start | bytes 196616 | tf_op jit(solution)/shard_map/ppermute | solution.py:287
  56.7 7.1 %collective-permute-start.16 = (bf16[64,512]{1,0:T(8,128)(2,1)S(1)}, bf16[64,512]{1,0:T(8,128)(2,1)S(1)}, u32[]{:S(2)}, u32[]{:S(2)}) collective-permute-start(bf16[64,512]{1,0:T(8,128)(2,1)S(1)} %add_convert_fusion.3), channel_id=1, source_target_pairs={{0,24},{8,0},{16,8},{24,16},{1,25},{9,1},{17,9},{25,17},{2,26},{10... | collective-permute-start | bytes 196616 | tf_op jit(solution)/shard_map/ppermute | solution.py:287
  58.3 5.5 %collective-permute-start.15 = (bf16[64,512]{1,0:T(8,128)(2,1)S(1)}, bf16[64,512]{1,0:T(8,128)(2,1)S(1)}, u32[]{:S(2)}, u32[]{:S(2)}) collective-permute-start(bf16[64,512]{1,0:T(8,128)(2,1)S(1)} %add_convert_fusion.3), channel_id=1, source_target_pairs={{0,16},{8,24},{16,0},{24,8},{1,17},{9,25},{17,1},{25,9},{2,18},{10... | collective-permute-start | bytes 196616 | tf_op jit(solution)/shard_map/ppermute | solution.py:287
  59.6 9.6 %collective-permute-start.10 = (bf16[320,384]{1,0:T(8,128)(2,1)S(1)}, bf16[320,384]{1,0:T(8,128)(2,1)S(1)}, u32[]{:S(2)}, u32[]{:S(2)}) collective-permute-start(bf16[320,384]{1,0:T(8,128)(2,1)S(1)} %add_convert_fusion.1), channel_id=1, source_target_pairs={{0,64},{64,128},{128,192},{192,0},{1,65},{65,129},{129,193},{193,1... | collective-permute-start | bytes 737288 | tf_op jit(solution)/shard_map/ppermute | solution.py:287
  60.8 8.4 %collective-permute-start.9 = (bf16[320,384]{1,0:T(8,128)(2,1)S(1)}, bf16[320,384]{1,0:T(8,128)(2,1)S(1)}, u32[]{:S(2)}, u32[]{:S(2)}) collective-permute-start(bf16[320,384]{1,0:T(8,128)(2,1)S(1)} %add_convert_fusion.1), channel_id=1, source_target_pairs={{0,192},{64,0},{128,64},{192,128},{1,193},{65,1},{129,65},{193,129... | collective-permute-start | bytes 737288 | tf_op jit(solution)/shard_map/ppermute | solution.py:287
  62.4 9.5 %collective-permute-start.8 = (bf16[320,384]{1,0:T(8,128)(2,1)S(1)}, bf16[320,384]{1,0:T(8,128)(2,1)S(1)}, u32[]{:S(2)}, u32[]{:S(2)}) collective-permute-start(bf16[320,384]{1,0:T(8,128)(2,1)S(1)} %add_convert_fusion.1), channel_id=1, source_target_pairs={{0,128},{64,192},{128,0},{192,64},{1,129},{65,193},{129,1},{193,65... | collective-permute-start | bytes 737288 | tf_op jit(solution)/shard_map/ppermute | solution.py:287
  69.2 9.4 %copy-start.4 = (bf16[576,896]{1,0:T(8,128)(2,1)S(1)}, bf16[576,896]{1,0:T(8,128)(2,1)}, u32[]{:S(2)}) copy-start(bf16[576,896]{1,0:T(8,128)(2,1)} %copy-done.3) | copy-start | bytes 3096580
  72.0 6.7 %collective-permute-start.21 = (bf16[320,384]{1,0:T(8,128)(2,1)S(1)}, bf16[320,384]{1,0:T(8,128)(2,1)S(1)}, u32[]{:S(2)}, u32[]{:S(2)}) collective-permute-start(bf16[320,384]{1,0:T(8,128)(2,1)S(1)} %add_convert_fusion.own_ref), channel_id=1, source_target_pairs={{0,32},{32,0},{1,33},{33,1},{2,34},{34,2},{3,35},{35,3},{4,36},{36... | collective-permute-start | bytes 737288 | tf_op jit(solution)/shard_map/ppermute | solution.py:287
  74.9 13.2 %collective-permute-start.20 = (bf16[192,512]{1,0:T(8,128)(2,1)S(1)}, bf16[192,512]{1,0:T(8,128)(2,1)S(1)}, u32[]{:S(2)}, u32[]{:S(2)}) collective-permute-start(bf16[192,512]{1,0:T(8,128)(2,1)S(1)} %pad_maximum_fusion.g0_ref), channel_id=1, source_target_pairs={{0,64},{64,128},{128,192},{192,0},{1,65},{65,129},{129,193},{193,1... | collective-permute-start | bytes 589832 | tf_op jit(solution)/shard_map/ppermute | solution.py:287
  75.9 12.2 %collective-permute-start.19 = (bf16[192,512]{1,0:T(8,128)(2,1)S(1)}, bf16[192,512]{1,0:T(8,128)(2,1)S(1)}, u32[]{:S(2)}, u32[]{:S(2)}) collective-permute-start(bf16[192,512]{1,0:T(8,128)(2,1)S(1)} %pad_maximum_fusion.g0_ref), channel_id=1, source_target_pairs={{0,128},{64,192},{128,0},{192,64},{1,129},{65,193},{129,1},{193,65... | collective-permute-start | bytes 589832 | tf_op jit(solution)/shard_map/ppermute | solution.py:287
  78.6 9.5 %collective-permute-start.18 = (bf16[192,512]{1,0:T(8,128)(2,1)S(1)}, bf16[192,512]{1,0:T(8,128)(2,1)S(1)}, u32[]{:S(2)}, u32[]{:S(2)}) collective-permute-start(bf16[192,512]{1,0:T(8,128)(2,1)S(1)} %pad_maximum_fusion.g0_ref), channel_id=1, source_target_pairs={{0,192},{64,0},{128,64},{192,128},{1,193},{65,1},{129,65},{193,129... | collective-permute-start | bytes 589832 | tf_op jit(solution)/shard_map/ppermute | solution.py:287
  84.1 10.5 %all-to-all-start.2 = ((bf16[8,16,1024]{2,1,0:T(8,128)(2,1)}), bf16[8,16,1024]{2,1,0:T(8,128)(2,1)S(1)}, u32[]{:S(2)}, u32[]{:S(2)}) async-start(bf16[8,16,1024]{2,1,0:T(8,128)(2,1)} %shard_map.82), calls=%async_computation.2 | async-start | bytes 524288 | tf_op jit(solution)/shard_map/all_to_all | solution.py:279

commit v2 on v1

--- a/solution.py
+++ b/solution.py
@@ -342,7 +342,7 @@
         *grads_b, grad_a
     )
     both = lax.all_gather(both, "c")
-    all_z, both = lax.optimization_barrier((all_z, both))
+    _, both = lax.optimization_barrier((all_z, both))
     all_a = others(all_z, "x", 4)
     moment_b, long_b, piece_b, grad_a = call(
         moment_b_body,

time: 95.8 us -> 95.8 us (level)
  no operation moved by 1% of the time
where the time goes in v2:
time: 95.8 us; the launch traced here: 95.4 us
  starting transfers between devices  52.6 us (55%)
  Pallas kernels  17 us (18%)
  waiting for transfers between devices  15.1 us (16%)
  blocking collectives  9.54 us (10%)
    ppermute x21, starting transfers between devices, shift(): return lax.ppermute(x, axis, [(i, (i + k) % n) for i in range(n)])  37.4 us
    all_to_all x3, starting transfers between devices, exchange(): return lax.all_to_all(x, axis, split_axis=0, concat_axis=0, tiled=True)  15.1 us
    all_to_all x3, waiting for transfers between devices, exchange(): return lax.all_to_all(x, axis, split_axis=0, concat_axis=0, tiled=True)  9.58 us
    ppermute x21, waiting for transfers between devices, shift(): return lax.ppermute(x, axis, [(i, (i + k) % n) for i in range(n)])  5.52 us
    pallas_call x1, Pallas kernels, local(): call(finish_a_body, shape((N_DP, MAIN, WIDE), bf16), 2, 3, [pltpu.VMEM((2...  5.52 us
    all_gather x1, blocking collectives, local(): piece_b = lax.all_gather(sum_over(piece_b, 'x', 4), 'c', tiled=True)  5.37 us
    pallas_call x1, Pallas kernels, local(): call(finish_b_body, shape(long_b.shape, bf16), 1, 5, [pltpu.VMEM((KV_RANK...  4.43 us
    all_gather x1, blocking collectives, local(): both = lax.all_gather(both, 'c')  4.17 us
  transfers between devices with their start and end apart: 25, of which 6 were waited for; matrix products, arithmetic and copies ran while one was open for 0% of the time, Pallas kernels for 14%

profile of v2, /device:TPU:1, one launch (start us, length us, event | category | flops | bytes accessed | tf_op | source)
XLA Modules:
  0.0 95.4 jit_solution(16216724329164234259)
XLA Ops:
  0.6 1.9 %shard_map.75 = (bf16[8,16,1024]{2,1,0:T(8,128)(2,1)}, bf16[256,512]{1,0:T(8,128)(2,1)}) custom-call(s32[1]{0:T(128)} %bitcast.1.c_ref, bf16[1,18,7168]{2,1,0:T(8,128)(2,1)} %a_ref.1, bf16[1,512,512]{2,1,0:T(8,128)(2,1)} %b_ref.3), custom_call_target="tpu_custom_call" | custom-call | tf_op jit(solution)/shard_map/pallas_call | solution.py:319
  2.5 0.0 copy-start.1
  2.5 3.3 %collective-permute-start = (bf16[256,512]{1,0:T(8,128)(2,1)}, bf16[256,512]{1,0:T(8,128)(2,1)S(1)}, u32[]{:S(2)}, u32[]{:S(2)}) collective-permute-start(bf16[256,512]{1,0:T(8,128)(2,1)} %get-tuple-element.25), channel_id=1, source_target_pairs={{0,32},{32,0},{1,33},{33,1},{2,34},{34,2},{3,35},{35,3},{4,36},{36... | collective-permute-start | bytes 786440 | tf_op jit(solution)/shard_map/ppermute | solution.py:287
  5.8 3.5 %all-to-all-start = ((bf16[8,16,1024]{2,1,0:T(8,128)(2,1)}), bf16[8,16,1024]{2,1,0:T(8,128)(2,1)S(1)}, u32[]{:S(2)}, u32[]{:S(2)}) async-start(bf16[8,16,1024]{2,1,0:T(8,128)(2,1)} %get-tuple-element.24), calls=%async_computation | async-start | bytes 524288 | tf_op jit(solution)/shard_map/all_to_all | solution.py:279
  9.3 0.0 collective-permute-done.x_ref
  9.4 0.1 shard_map.76.b0_ref
  9.4 6.4 %all-to-all-done.parts_ref = bf16[8,16,1024]{2,1,0:T(8,128)(2,1)S(1)} async-done(((bf16[8,16,1024]{2,1,0:T(8,128)(2,1)}), bf16[8,16,1024]{2,1,0:T(8,128)(2,1)S(1)}, u32[]{:S(2)}, u32[]{:S(2)}) %all-to-all-start) | async-done | bytes 262176 | tf_op jit(solution)/shard_map/all_to_all | solution.py:279
  15.8 0.3 collective-permute-start.10
  16.1 1.8 %collective-permute-start.9 = (bf16[256,512]{1,0:T(8,128)(2,1)S(1)}, bf16[256,512]{1,0:T(8,128)(2,1)S(1)}, u32[]{:S(2)}, u32[]{:S(2)}) collective-permute-start(bf16[256,512]{1,0:T(8,128)(2,1)S(1)} %shard_map.76.b0_ref), channel_id=1, source_target_pairs={{0,128},{64,192},{128,0},{192,64},{1,129},{65,193},{129,1},{193,65... | collective-permute-start | bytes 786440 | tf_op jit(solution)/shard_map/ppermute | solution.py:287
  17.9 0.6 collective-permute-start.8
  18.5 0.8 shard_map.77
  19.3 7.7 %all-to-all-start.1 = ((bf16[8,16,1024]{2,1,0:T(8,128)(2,1)}), bf16[8,16,1024]{2,1,0:T(8,128)(2,1)S(1)}, u32[]{:S(2)}, u32[]{:S(2)}) async-start(bf16[8,16,1024]{2,1,0:T(8,128)(2,1)} %get-tuple-element.27), calls=%async_computation.1 | async-start | bytes 524288 | tf_op jit(solution)/shard_map/all_to_all | solution.py:279
  27.0 0.0 collective-permute-done.10.b3_ref
  27.0 1.9 %collective-permute-done.9.b2_ref = bf16[256,512]{1,0:T(8,128)(2,1)S(1)} collective-permute-done((bf16[256,512]{1,0:T(8,128)(2,1)S(1)}, bf16[256,512]{1,0:T(8,128)(2,1)S(1)}, u32[]{:S(2)}, u32[]{:S(2)}) %collective-permute-start.9) | collective-permute-done | bytes 262176 | tf_op jit(solution)/shard_map/ppermute | solution.py:287
  28.9 1.0 %collective-permute-done.8.b1_ref = bf16[256,512]{1,0:T(8,128)(2,1)S(1)} collective-permute-done((bf16[256,512]{1,0:T(8,128)(2,1)S(1)}, bf16[256,512]{1,0:T(8,128)(2,1)S(1)}, u32[]{:S(2)}, u32[]{:S(2)}) %collective-permute-start.8) | collective-permute-done | bytes 262176 | tf_op jit(solution)/shard_map/ppermute | solution.py:287
  29.8 0.1 shard_map.79
  30.0 4.2 %all-gather = bf16[576,512]{1,0:T(8,128)(2,1)S(1)} all-gather(bf16[288,512]{1,0:T(8,128)(2,1)S(1)} %shard_map.79), channel_id=2, replica_groups=mesh['y'=4,'c'=2,'x'=4,'z'=8] {'c'}, dimensions={0}, use_global_device_ids=true | all-gather | bytes 884736 | tf_op jit(solution)/shard_map/all_gather | solution.py:344
  34.1 2.1 %all-to-all-done.1.x0_ref = bf16[8,16,1024]{2,1,0:T(8,128)(2,1)S(1)} async-done(((bf16[8,16,1024]{2,1,0:T(8,128)(2,1)}), bf16[8,16,1024]{2,1,0:T(8,128)(2,1)S(1)}, u32[]{:S(2)}, u32[]{:S(2)}) %all-to-all-start.1) | async-done | bytes 262176 | tf_op jit(solution)/shard_map/all_to_all | solution.py:279
  36.2 1.2 %shard_map.80 = (f32[512,512]{1,0:T(8,128)}, bf16[512,512]{1,0:T(8,128)(2,1)S(1)}, bf16[64,512]{1,0:T(8,128)(2,1)S(1)}, bf16[2,32,512]{2,1,0:T(8,128)(2,1)S(1)}) custom-call(s32[1]{0:T(128)S(6)} %add.36.d_ref, bf16[2,288,512]{2,1,0:T(8,128)(2,1)S(1)} %bitcast.5, f32[512,512]{1,0:T(8,128)S(1)} %copy-done.2), custom_call_target="tpu_custom_call" | custom-call | tf_op jit(solution)/shard_map/pallas_call | solution.py:347
  37.4 0.1 collective-permute-start.11
  37.5 1.2 %collective-permute-start.3 = (bf16[8,16,1024]{2,1,0:T(8,128)(2,1)S(1)}, bf16[8,16,1024]{2,1,0:T(8,128)(2,1)S(1)}, u32[]{:S(2)}, u32[]{:S(2)}) collective-permute-start(bf16[8,16,1024]{2,1,0:T(8,128)(2,1)S(1)} %all-to-all-done.1.x0_ref), channel_id=1, source_target_pairs={{0,8},{8,16},{16,24},{24,0},{1,9},{9,17},{17,25},{25,1},{2,10},{10... | collective-permute-start | bytes 786440 | tf_op jit(solution)/shard_map/ppermute | solution.py:287
  38.7 2.4 %collective-permute-start.2 = (bf16[8,16,1024]{2,1,0:T(8,128)(2,1)S(1)}, bf16[8,16,1024]{2,1,0:T(8,128)(2,1)S(1)}, u32[]{:S(2)}, u32[]{:S(2)}) collective-permute-start(bf16[8,16,1024]{2,1,0:T(8,128)(2,1)S(1)} %all-to-all-done.1.x0_ref), channel_id=1, source_target_pairs={{0,16},{8,24},{16,0},{24,8},{1,17},{9,25},{17,1},{25,9},{2,18},{10... | collective-permute-start | bytes 786440 | tf_op jit(solution)/shard_map/ppermute | solution.py:287
  41.2 1.2 %collective-permute-start.1 = (bf16[8,16,1024]{2,1,0:T(8,128)(2,1)S(1)}, bf16[8,16,1024]{2,1,0:T(8,128)(2,1)S(1)}, u32[]{:S(2)}, u32[]{:S(2)}) collective-permute-start(bf16[8,16,1024]{2,1,0:T(8,128)(2,1)S(1)} %all-to-all-done.1.x0_ref), channel_id=1, source_target_pairs={{0,24},{8,0},{16,8},{24,16},{1,25},{9,1},{17,9},{25,17},{2,26},{10... | collective-permute-start | bytes 786440 | tf_op jit(solution)/shard_map/ppermute | solution.py:287
  42.3 2.0 %collective-permute-start.14 = (bf16[64,512]{1,0:T(8,128)(2,1)S(1)}, bf16[64,512]{1,0:T(8,128)(2,1)S(1)}, u32[]{:S(2)}, u32[]{:S(2)}) collective-permute-start(bf16[64,512]{1,0:T(8,128)(2,1)S(1)} %add_convert_fusion.4), channel_id=1, source_target_pairs={{0,2},{1,3},{2,4},{3,5},{4,6},{5,7},{6,0},{7,1},{8,10},{9,11},{10,... | collective-permute-start | bytes 196616 | tf_op jit(solution)/shard_map/ppermute | solution.py:287
  44.4 4.2 %collective-permute-start.13 = (bf16[64,512]{1,0:T(8,128)(2,1)S(1)}, bf16[64,512]{1,0:T(8,128)(2,1)S(1)}, u32[]{:S(2)}, u32[]{:S(2)}) collective-permute-start(bf16[64,512]{1,0:T(8,128)(2,1)S(1)} %add_convert_fusion.4), channel_id=1, source_target_pairs={{0,4},{1,5},{2,6},{3,7},{4,0},{5,1},{6,2},{7,3},{8,12},{9,13},{10,... | collective-permute-start | bytes 196616 | tf_op jit(solution)/shard_map/ppermute | solution.py:287
  48.6 0.0 collective-permute-done.3.x3_ref
  48.6 2.4 %collective-permute-start.12 = (bf16[64,512]{1,0:T(8,128)(2,1)S(1)}, bf16[64,512]{1,0:T(8,128)(2,1)S(1)}, u32[]{:S(2)}, u32[]{:S(2)}) collective-permute-start(bf16[64,512]{1,0:T(8,128)(2,1)S(1)} %add_convert_fusion.4), channel_id=1, source_target_pairs={{0,6},{1,7},{2,0},{3,1},{4,2},{5,3},{6,4},{7,5},{8,14},{9,15},{10,... | collective-permute-start | bytes 196616 | tf_op jit(solution)/shard_map/ppermute | solution.py:287
  51.0 1.4 %shard_map.78 = (bf16[320,384]{1,0:T(8,128)(2,1)S(1)}, bf16[320,384]{1,0:T(8,128)(2,1)S(1)}, bf16[576,896]{1,0:T(8,128)(2,1)S(1)}) custom-call(s32[1]{0:T(128)} %bitcast.1.c_ref, bf16[8,16,1024]{2,1,0:T(8,128)(2,1)S(1)} %all-to-all-done.1.x0_ref, bf16[8,16,1024]{2,1,0:T(8,128)(2,1)S(1)} %collective-permute-done.1.x1_ref, ...), custom_call_target="tpu_custom_call" | custom-call | tf_op jit(solution)/shard_map/pallas_call | solution.py:362
  52.4 3.1 %collective-permute-start.4 = (bf16[320,384]{1,0:T(8,128)(2,1)S(1)}, bf16[320,384]{1,0:T(8,128)(2,1)S(1)}, u32[]{:S(2)}, u32[]{:S(2)}) collective-permute-start(bf16[320,384]{1,0:T(8,128)(2,1)S(1)} %get-tuple-element.29), channel_id=1, source_target_pairs={{0,32},{32,0},{1,33},{33,1},{2,34},{34,2},{3,35},{35,3},{4,36},{36... | collective-permute-start | bytes 737288 | tf_op jit(solution)/shard_map/ppermute | solution.py:287
  55.6 1.1 %collective-permute-start.17 = (bf16[64,512]{1,0:T(8,128)(2,1)S(1)}, bf16[64,512]{1,0:T(8,128)(2,1)S(1)}, u32[]{:S(2)}, u32[]{:S(2)}) collective-permute-start(bf16[64,512]{1,0:T(8,128)(2,1)S(1)} %add_convert_fusion.3), channel_id=1, source_target_pairs={{0,8},{8,16},{16,24},{24,0},{1,9},{9,17},{17,25},{25,1},{2,10},{10... | collective-permute-start | bytes 196616 | tf_op jit(solution)/shard_map/ppermute | solution.py:287
  56.7 1.6 %collective-permute-start.16 = (bf16[64,512]{1,0:T(8,128)(2,1)S(1)}, bf16[64,512]{1,0:T(8,128)(2,1)S(1)}, u32[]{:S(2)}, u32[]{:S(2)}) collective-permute-start(bf16[64,512]{1,0:T(8,128)(2,1)S(1)} %add_convert_fusion.3), channel_id=1, source_target_pairs={{0,24},{8,0},{16,8},{24,16},{1,25},{9,1},{17,9},{25,17},{2,26},{10... | collective-permute-start | bytes 196616 | tf_op jit(solution)/shard_map/ppermute | solution.py:287
  58.3 1.2 %collective-permute-start.15 = (bf16[64,512]{1,0:T(8,128)(2,1)S(1)}, bf16[64,512]{1,0:T(8,128)(2,1)S(1)}, u32[]{:S(2)}, u32[]{:S(2)}) collective-permute-start(bf16[64,512]{1,0:T(8,128)(2,1)S(1)} %add_convert_fusion.3), channel_id=1, source_target_pairs={{0,16},{8,24},{16,0},{24,8},{1,17},{9,25},{17,1},{25,9},{2,18},{10... | collective-permute-start | bytes 196616 | tf_op jit(solution)/shard_map/ppermute | solution.py:287
  59.5 0.1 add_convert_fusion.1
  59.6 1.2 %collective-permute-start.7 = (bf16[320,384]{1,0:T(8,128)(2,1)S(1)}, bf16[320,384]{1,0:T(8,128)(2,1)S(1)}, u32[]{:S(2)}, u32[]{:S(2)}) collective-permute-start(bf16[320,384]{1,0:T(8,128)(2,1)S(1)} %add_convert_fusion.1), channel_id=1, source_target_pairs={{0,64},{64,128},{128,192},{192,0},{1,65},{65,129},{129,193},{193,1... | collective-permute-start | bytes 737288 | tf_op jit(solution)/shard_map/ppermute | solution.py:287
  60.8 1.5 %collective-permute-start.6 = (bf16[320,384]{1,0:T(8,128)(2,1)S(1)}, bf16[320,384]{1,0:T(8,128)(2,1)S(1)}, u32[]{:S(2)}, u32[]{:S(2)}) collective-permute-start(bf16[320,384]{1,0:T(8,128)(2,1)S(1)} %add_convert_fusion.1), channel_id=1, source_target_pairs={{0,192},{64,0},{128,64},{192,128},{1,193},{65,1},{129,65},{193,129... | collective-permute-start | bytes 737288 | tf_op jit(solution)/shard_map/ppermute | solution.py:287
  62.4 1.4 %collective-permute-start.5 = (bf16[320,384]{1,0:T(8,128)(2,1)S(1)}, bf16[320,384]{1,0:T(8,128)(2,1)S(1)}, u32[]{:S(2)}, u32[]{:S(2)}) collective-permute-start(bf16[320,384]{1,0:T(8,128)(2,1)S(1)} %add_convert_fusion.1), channel_id=1, source_target_pairs={{0,128},{64,192},{128,0},{192,64},{1,129},{65,193},{129,1},{193,65... | collective-permute-start | bytes 737288 | tf_op jit(solution)/shard_map/ppermute | solution.py:287
  63.8 5.4 %all_gather.11 = bf16[128,512]{1,0:T(8,128)(2,1)S(1)} all-gather(bf16[64,512]{1,0:T(8,128)(2,1)S(1)} %add_convert_fusion.2), channel_id=1, replica_groups=mesh['y'=4,'c'=2,'x'=4,'z'=8] {'c'}, dimensions={0}, use_global_device_ids=true | all-gather | bytes 196608 | tf_op jit(solution)/shard_map/all_gather | solution.py:373
  69.2 2.6 %collective-permute-done.5 = bf16[320,384]{1,0:T(8,128)(2,1)S(1)} collective-permute-done((bf16[320,384]{1,0:T(8,128)(2,1)S(1)}, bf16[320,384]{1,0:T(8,128)(2,1)S(1)}, u32[]{:S(2)}, u32[]{:S(2)}) %collective-permute-start.5) | collective-permute-done | bytes 245792 | tf_op jit(solution)/shard_map/ppermute | solution.py:287
  71.8 0.1 add_convert_fusion.own_ref
  72.0 2.9 %collective-permute-start.21 = (bf16[320,384]{1,0:T(8,128)(2,1)S(1)}, bf16[320,384]{1,0:T(8,128)(2,1)S(1)}, u32[]{:S(2)}, u32[]{:S(2)}) collective-permute-start(bf16[320,384]{1,0:T(8,128)(2,1)S(1)} %add_convert_fusion.own_ref), channel_id=1, source_target_pairs={{0,32},{32,0},{1,33},{33,1},{2,34},{34,2},{3,35},{35,3},{4,36},{36... | collective-permute-start | bytes 737288 | tf_op jit(solution)/shard_map/ppermute | solution.py:287
  74.9 1.0 %collective-permute-start.20 = (bf16[192,512]{1,0:T(8,128)(2,1)S(1)}, bf16[192,512]{1,0:T(8,128)(2,1)S(1)}, u32[]{:S(2)}, u32[]{:S(2)}) collective-permute-start(bf16[192,512]{1,0:T(8,128)(2,1)S(1)} %pad_maximum_fusion.g0_ref), channel_id=1, source_target_pairs={{0,64},{64,128},{128,192},{192,0},{1,65},{65,129},{129,193},{193,1... | collective-permute-start | bytes 589832 | tf_op jit(solution)/shard_map/ppermute | solution.py:287
  75.9 2.8 %collective-permute-start.19 = (bf16[192,512]{1,0:T(8,128)(2,1)S(1)}, bf16[192,512]{1,0:T(8,128)(2,1)S(1)}, u32[]{:S(2)}, u32[]{:S(2)}) collective-permute-start(bf16[192,512]{1,0:T(8,128)(2,1)S(1)} %pad_maximum_fusion.g0_ref), channel_id=1, source_target_pairs={{0,128},{64,192},{128,0},{192,64},{1,129},{65,193},{129,1},{193,65... | collective-permute-start | bytes 589832 | tf_op jit(solution)/shard_map/ppermute | solution.py:287
  78.6 5.5 %shard_map.82 = bf16[8,16,1024]{2,1,0:T(8,128)(2,1)} custom-call(s32[1]{0:T(128)} %bitcast.4.f_ref, s32[1]{0:T(128)} %bitcast.1.c_ref, bf16[320,384]{1,0:T(8,128)(2,1)S(1)} %add_convert_fusion.own_ref, bf16[320,384]{1,0:T(8,128)(2,1)S(1)} %collective-permute-done.21.other_ref, bf16[576,896]{1,0:T(8,128)(2,1)S(1)} %copy-done.4), custom_call_target="tpu_custom_call" | custom-call | flops 40000000000 | tf_op jit(solution)/shard_map/pallas_call | solution.py:379
  84.1 4.0 %all-to-all-start.2 = ((bf16[8,16,1024]{2,1,0:T(8,128)(2,1)}), bf16[8,16,1024]{2,1,0:T(8,128)(2,1)S(1)}, u32[]{:S(2)}, u32[]{:S(2)}) async-start(bf16[8,16,1024]{2,1,0:T(8,128)(2,1)} %shard_map.82), calls=%async_computation.2 | async-start | bytes 524288 | tf_op jit(solution)/shard_map/all_to_all | solution.py:279
  88.1 4.4 %shard_map.84 = bf16[512,512]{1,0:T(8,128)(2,1)} custom-call(s32[1]{0:T(128)} %bitcast.i_ref, bf16[192,512]{1,0:T(8,128)(2,1)S(1)} %pad_maximum_fusion.g0_ref, bf16[192,512]{1,0:T(8,128)(2,1)S(1)} %collective-permute-done.18.g1_ref, bf16[192,512]{1,0:T(8,128)(2,1)S(1)} %collective-permute-done.19.g2_ref, ...), custom_call_target="tpu_custom_call" | custom-call | flops 40000000000 | tf_op jit(solution)/shard_map/pallas_call | solution.py:390
  92.5 1.0 %shard_map.81 = f32[18,7168]{1,0:T(8,128)} custom-call(s32[1]{0:T(128)} %bitcast.i_ref, bf16[192,512]{1,0:T(8,128)(2,1)S(1)} %pad_maximum_fusion.g0_ref, bf16[192,512]{1,0:T(8,128)(2,1)S(1)} %collective-permute-done.18.g1_ref, bf16[192,512]{1,0:T(8,128)(2,1)S(1)} %collective-permute-done.19.g2_ref, bf16[192,512]{1,0:T(8,128)(2,1)S(1)} %collective-permute-done.20.g3_ref, ...), custom_call_target="tpu_custom_call" | custom-call | tf_op jit(solution)/shard_map/pallas_call | solution.py:388
  93.5 1.1 %all-to-all-done.2.u_ref = bf16[8,16,1024]{2,1,0:T(8,128)(2,1)S(1)} async-done(((bf16[8,16,1024]{2,1,0:T(8,128)(2,1)}), bf16[8,16,1024]{2,1,0:T(8,128)(2,1)S(1)}, u32[]{:S(2)}, u32[]{:S(2)}) %all-to-all-start.2) | async-done | bytes 262176 | tf_op jit(solution)/shard_map/all_to_all | solution.py:279
  94.6 0.8 shard_map.83
  (30 shorter events, 0.2 us)
Async XLA Ops:
  2.5 6.9 %copy-start.1 = (bf16[1,512,512]{2,1,0:T(8,128)(2,1)S(1)}, bf16[1,512,512]{2,1,0:T(8,128)(2,1)}, u32[]{:S(2)}) copy-start(bf16[1,512,512]{2,1,0:T(8,128)(2,1)} %b_ref.3) | copy-start | bytes 1572868
  2.5 6.8 %collective-permute-start = (bf16[256,512]{1,0:T(8,128)(2,1)}, bf16[256,512]{1,0:T(8,128)(2,1)S(1)}, u32[]{:S(2)}, u32[]{:S(2)}) collective-permute-start(bf16[256,512]{1,0:T(8,128)(2,1)} %get-tuple-element.25), channel_id=1, source_target_pairs={{0,32},{32,0},{1,33},{33,1},{2,34},{34,2},{3,35},{35,3},{4,36},{36... | collective-permute-start | bytes 786440 | tf_op jit(solution)/shard_map/ppermute | solution.py:287
  5.8 12.7 %copy-start = (f32[18,7168]{1,0:T(8,128)S(1)}, f32[18,7168]{1,0:T(8,128)}, u32[]{:S(2)}) copy-start(f32[18,7168]{1,0:T(8,128)} %m_ref.5) | copy-start | bytes 1548292
  5.8 10.0 %all-to-all-start = ((bf16[8,16,1024]{2,1,0:T(8,128)(2,1)}), bf16[8,16,1024]{2,1,0:T(8,128)(2,1)S(1)}, u32[]{:S(2)}, u32[]{:S(2)}) async-start(bf16[8,16,1024]{2,1,0:T(8,128)(2,1)} %get-tuple-element.24), calls=%async_computation | async-start | bytes 524288 | tf_op jit(solution)/shard_map/all_to_all | solution.py:279
  15.8 11.1 %collective-permute-start.10 = (bf16[256,512]{1,0:T(8,128)(2,1)S(1)}, bf16[256,512]{1,0:T(8,128)(2,1)S(1)}, u32[]{:S(2)}, u32[]{:S(2)}) collective-permute-start(bf16[256,512]{1,0:T(8,128)(2,1)S(1)} %shard_map.76.b0_ref), channel_id=1, source_target_pairs={{0,64},{64,128},{128,192},{192,0},{1,65},{65,129},{129,193},{193,1... | collective-permute-start | bytes 786440 | tf_op jit(solution)/shard_map/ppermute | solution.py:287
  16.1 12.7 %collective-permute-start.9 = (bf16[256,512]{1,0:T(8,128)(2,1)S(1)}, bf16[256,512]{1,0:T(8,128)(2,1)S(1)}, u32[]{:S(2)}, u32[]{:S(2)}) collective-permute-start(bf16[256,512]{1,0:T(8,128)(2,1)S(1)} %shard_map.76.b0_ref), channel_id=1, source_target_pairs={{0,128},{64,192},{128,0},{192,64},{1,129},{65,193},{129,1},{193,65... | collective-permute-start | bytes 786440 | tf_op jit(solution)/shard_map/ppermute | solution.py:287
  17.9 11.9 %collective-permute-start.8 = (bf16[256,512]{1,0:T(8,128)(2,1)S(1)}, bf16[256,512]{1,0:T(8,128)(2,1)S(1)}, u32[]{:S(2)}, u32[]{:S(2)}) collective-permute-start(bf16[256,512]{1,0:T(8,128)(2,1)S(1)} %shard_map.76.b0_ref), channel_id=1, source_target_pairs={{0,192},{64,0},{128,64},{192,128},{1,193},{65,1},{129,65},{193,129... | collective-permute-start | bytes 786440 | tf_op jit(solution)/shard_map/ppermute | solution.py:287
  19.3 16.9 %all-to-all-start.1 = ((bf16[8,16,1024]{2,1,0:T(8,128)(2,1)}), bf16[8,16,1024]{2,1,0:T(8,128)(2,1)S(1)}, u32[]{:S(2)}, u32[]{:S(2)}) async-start(bf16[8,16,1024]{2,1,0:T(8,128)(2,1)} %get-tuple-element.27), calls=%async_computation.1 | async-start | bytes 524288 | tf_op jit(solution)/shard_map/all_to_all | solution.py:279
  29.8 6.4 %copy-start.2 = (f32[512,512]{1,0:T(8,128)S(1)}, f32[512,512]{1,0:T(8,128)}, u32[]{:S(2)}) copy-start(f32[512,512]{1,0:T(8,128)} %m_ref.4) | copy-start | bytes 3145732
  37.4 4.9 %collective-permute-start.11 = (bf16[64,512]{1,0:T(8,128)(2,1)S(1)}, bf16[64,512]{1,0:T(8,128)(2,1)S(1)}, u32[]{:S(2)}, u32[]{:S(2)}) collective-permute-start(bf16[64,512]{1,0:T(8,128)(2,1)S(1)} %get-tuple-element.33), channel_id=1, source_target_pairs={{0,1},{1,0},{2,3},{3,2},{4,5},{5,4},{6,7},{7,6},{8,9},{9,8},{10,11... | collective-permute-start | bytes 196616 | tf_op jit(solution)/shard_map/ppermute | solution.py:307
  37.5 11.1 %collective-permute-start.3 = (bf16[8,16,1024]{2,1,0:T(8,128)(2,1)S(1)}, bf16[8,16,1024]{2,1,0:T(8,128)(2,1)S(1)}, u32[]{:S(2)}, u32[]{:S(2)}) collective-permute-start(bf16[8,16,1024]{2,1,0:T(8,128)(2,1)S(1)} %all-to-all-done.1.x0_ref), channel_id=1, source_target_pairs={{0,8},{8,16},{16,24},{24,0},{1,9},{9,17},{17,25},{25,1},{2,10},{10... | collective-permute-start | bytes 786440 | tf_op jit(solution)/shard_map/ppermute | solution.py:287
  38.7 12.3 %collective-permute-start.2 = (bf16[8,16,1024]{2,1,0:T(8,128)(2,1)S(1)}, bf16[8,16,1024]{2,1,0:T(8,128)(2,1)S(1)}, u32[]{:S(2)}, u32[]{:S(2)}) collective-permute-start(bf16[8,16,1024]{2,1,0:T(8,128)(2,1)S(1)} %all-to-all-done.1.x0_ref), channel_id=1, source_target_pairs={{0,16},{8,24},{16,0},{24,8},{1,17},{9,25},{17,1},{25,9},{2,18},{10... | collective-permute-start | bytes 786440 | tf_op jit(solution)/shard_map/ppermute | solution.py:287
  41.2 9.8 %collective-permute-start.1 = (bf16[8,16,1024]{2,1,0:T(8,128)(2,1)S(1)}, bf16[8,16,1024]{2,1,0:T(8,128)(2,1)S(1)}, u32[]{:S(2)}, u32[]{:S(2)}) collective-permute-start(bf16[8,16,1024]{2,1,0:T(8,128)(2,1)S(1)} %all-to-all-done.1.x0_ref), channel_id=1, source_target_pairs={{0,24},{8,0},{16,8},{24,16},{1,25},{9,1},{17,9},{25,17},{2,26},{10... | collective-permute-start | bytes 786440 | tf_op jit(solution)/shard_map/ppermute | solution.py:287
  42.3 13.2 %collective-permute-start.14 = (bf16[64,512]{1,0:T(8,128)(2,1)S(1)}, bf16[64,512]{1,0:T(8,128)(2,1)S(1)}, u32[]{:S(2)}, u32[]{:S(2)}) collective-permute-start(bf16[64,512]{1,0:T(8,128)(2,1)S(1)} %add_convert_fusion.4), channel_id=1, source_target_pairs={{0,2},{1,3},{2,4},{3,5},{4,6},{5,7},{6,0},{7,1},{8,10},{9,11},{10,... | collective-permute-start | bytes 196616 | tf_op jit(solution)/shard_map/ppermute | solution.py:287
  44.4 11.1 %collective-permute-start.13 = (bf16[64,512]{1,0:T(8,128)(2,1)S(1)}, bf16[64,512]{1,0:T(8,128)(2,1)S(1)}, u32[]{:S(2)}, u32[]{:S(2)}) collective-permute-start(bf16[64,512]{1,0:T(8,128)(2,1)S(1)} %add_convert_fusion.4), channel_id=1, source_target_pairs={{0,4},{1,5},{2,6},{3,7},{4,0},{5,1},{6,2},{7,3},{8,12},{9,13},{10,... | collective-permute-start | bytes 196616 | tf_op jit(solution)/shard_map/ppermute | solution.py:287
  48.6 6.9 %collective-permute-start.12 = (bf16[64,512]{1,0:T(8,128)(2,1)S(1)}, bf16[64,512]{1,0:T(8,128)(2,1)S(1)}, u32[]{:S(2)}, u32[]{:S(2)}) collective-permute-start(bf16[64,512]{1,0:T(8,128)(2,1)S(1)} %add_convert_fusion.4), channel_id=1, source_target_pairs={{0,6},{1,7},{2,0},{3,1},{4,2},{5,3},{6,4},{7,5},{8,14},{9,15},{10,... | collective-permute-start | bytes 196616 | tf_op jit(solution)/shard_map/ppermute | solution.py:287
  52.4 16.8 %copy-start.3 = (bf16[576,896]{1,0:T(8,128)(2,1)}, bf16[576,896]{1,0:T(8,128)(2,1)S(1)}, u32[]{:S(2)}) copy-start(bf16[576,896]{1,0:T(8,128)(2,1)S(1)} %get-tuple-element.42.x_ref) | copy-start | bytes 3096580
  52.4 7.2 %collective-permute-start.4 = (bf16[320,384]{1,0:T(8,128)(2,1)S(1)}, bf16[320,384]{1,0:T(8,128)(2,1)S(1)}, u32[]{:S(2)}, u32[]{:S(2)}) collective-permute-start(bf16[320,384]{1,0:T(8,128)(2,1)S(1)} %get-tuple-element.29), channel_id=1, source_target_pairs={{0,32},{32,0},{1,33},{33,1},{2,34},{34,2},{3,35},{35,3},{4,36},{36... | collective-permute-start | bytes 737288 | tf_op jit(solution)/shard_map/ppermute | solution.py:287
  55.6 6.8 %collective-permute-start.17 = (bf16[64,512]{1,0:T(8,128)(2,1)S(1)}, bf16[64,512]{1,0:T(8,128)(2,1)S(1)}, u32[]{:S(2)}, u32[]{:S(2)}) collective-permute-start(bf16[64,512]{1,0:T(8,128)(2,1)S(1)} %add_convert_fusion.3), channel_id=1, source_target_pairs={{0,8},{8,16},{16,24},{24,0},{1,9},{9,17},{17,25},{25,1},{2,10},{10... | collective-permute-start | bytes 196616 | tf_op jit(solution)/shard_map/ppermute | solution.py:287
  56.7 7.1 %collective-permute-start.16 = (bf16[64,512]{1,0:T(8,128)(2,1)S(1)}, bf16[64,512]{1,0:T(8,128)(2,1)S(1)}, u32[]{:S(2)}, u32[]{:S(2)}) collective-permute-start(bf16[64,512]{1,0:T(8,128)(2,1)S(1)} %add_convert_fusion.3), channel_id=1, source_target_pairs={{0,24},{8,0},{16,8},{24,16},{1,25},{9,1},{17,9},{25,17},{2,26},{10... | collective-permute-start | bytes 196616 | tf_op jit(solution)/shard_map/ppermute | solution.py:287
  58.3 5.5 %collective-permute-start.15 = (bf16[64,512]{1,0:T(8,128)(2,1)S(1)}, bf16[64,512]{1,0:T(8,128)(2,1)S(1)}, u32[]{:S(2)}, u32[]{:S(2)}) collective-permute-start(bf16[64,512]{1,0:T(8,128)(2,1)S(1)} %add_convert_fusion.3), channel_id=1, source_target_pairs={{0,16},{8,24},{16,0},{24,8},{1,17},{9,25},{17,1},{25,9},{2,18},{10... | collective-permute-start | bytes 196616 | tf_op jit(solution)/shard_map/ppermute | solution.py:287
  59.6 9.6 %collective-permute-start.7 = (bf16[320,384]{1,0:T(8,128)(2,1)S(1)}, bf16[320,384]{1,0:T(8,128)(2,1)S(1)}, u32[]{:S(2)}, u32[]{:S(2)}) collective-permute-start(bf16[320,384]{1,0:T(8,128)(2,1)S(1)} %add_convert_fusion.1), channel_id=1, source_target_pairs={{0,64},{64,128},{128,192},{192,0},{1,65},{65,129},{129,193},{193,1... | collective-permute-start | bytes 737288 | tf_op jit(solution)/shard_map/ppermute | solution.py:287
  60.8 8.4 %collective-permute-start.6 = (bf16[320,384]{1,0:T(8,128)(2,1)S(1)}, bf16[320,384]{1,0:T(8,128)(2,1)S(1)}, u32[]{:S(2)}, u32[]{:S(2)}) collective-permute-start(bf16[320,384]{1,0:T(8,128)(2,1)S(1)} %add_convert_fusion.1), channel_id=1, source_target_pairs={{0,192},{64,0},{128,64},{192,128},{1,193},{65,1},{129,65},{193,129... | collective-permute-start | bytes 737288 | tf_op jit(solution)/shard_map/ppermute | solution.py:287
  62.4 9.5 %collective-permute-start.5 = (bf16[320,384]{1,0:T(8,128)(2,1)S(1)}, bf16[320,384]{1,0:T(8,128)(2,1)S(1)}, u32[]{:S(2)}, u32[]{:S(2)}) collective-permute-start(bf16[320,384]{1,0:T(8,128)(2,1)S(1)} %add_convert_fusion.1), channel_id=1, source_target_pairs={{0,128},{64,192},{128,0},{192,64},{1,129},{65,193},{129,1},{193,65... | collective-permute-start | bytes 737288 | tf_op jit(solution)/shard_map/ppermute | solution.py:287
  69.2 9.4 %copy-start.4 = (bf16[576,896]{1,0:T(8,128)(2,1)S(1)}, bf16[576,896]{1,0:T(8,128)(2,1)}, u32[]{:S(2)}) copy-start(bf16[576,896]{1,0:T(8,128)(2,1)} %copy-done.3) | copy-start | bytes 3096580
  72.0 6.7 %collective-permute-start.21 = (bf16[320,384]{1,0:T(8,128)(2,1)S(1)}, bf16[320,384]{1,0:T(8,128)(2,1)S(1)}, u32[]{:S(2)}, u32[]{:S(2)}) collective-permute-start(bf16[320,384]{1,0:T(8,128)(2,1)S(1)} %add_convert_fusion.own_ref), channel_id=1, source_target_pairs={{0,32},{32,0},{1,33},{33,1},{2,34},{34,2},{3,35},{35,3},{4,36},{36... | collective-permute-start | bytes 737288 | tf_op jit(solution)/shard_map/ppermute | solution.py:287
  74.9 13.2 %collective-permute-start.20 = (bf16[192,512]{1,0:T(8,128)(2,1)S(1)}, bf16[192,512]{1,0:T(8,128)(2,1)S(1)}, u32[]{:S(2)}, u32[]{:S(2)}) collective-permute-start(bf16[192,512]{1,0:T(8,128)(2,1)S(1)} %pad_maximum_fusion.g0_ref), channel_id=1, source_target_pairs={{0,64},{64,128},{128,192},{192,0},{1,65},{65,129},{129,193},{193,1... | collective-permute-start | bytes 589832 | tf_op jit(solution)/shard_map/ppermute | solution.py:287
  75.9 12.2 %collective-permute-start.19 = (bf16[192,512]{1,0:T(8,128)(2,1)S(1)}, bf16[192,512]{1,0:T(8,128)(2,1)S(1)}, u32[]{:S(2)}, u32[]{:S(2)}) collective-permute-start(bf16[192,512]{1,0:T(8,128)(2,1)S(1)} %pad_maximum_fusion.g0_ref), channel_id=1, source_target_pairs={{0,128},{64,192},{128,0},{192,64},{1,129},{65,193},{129,1},{193,65... | collective-permute-start | bytes 589832 | tf_op jit(solution)/shard_map/ppermute | solution.py:287
  78.6 9.5 %collective-permute-start.18 = (bf16[192,512]{1,0:T(8,128)(2,1)S(1)}, bf16[192,512]{1,0:T(8,128)(2,1)S(1)}, u32[]{:S(2)}, u32[]{:S(2)}) collective-permute-start(bf16[192,512]{1,0:T(8,128)(2,1)S(1)} %pad_maximum_fusion.g0_ref), channel_id=1, source_target_pairs={{0,192},{64,0},{128,64},{192,128},{1,193},{65,1},{129,65},{193,129... | collective-permute-start | bytes 589832 | tf_op jit(solution)/shard_map/ppermute | solution.py:287
  84.1 10.5 %all-to-all-start.2 = ((bf16[8,16,1024]{2,1,0:T(8,128)(2,1)}), bf16[8,16,1024]{2,1,0:T(8,128)(2,1)S(1)}, u32[]{:S(2)}, u32[]{:S(2)}) async-start(bf16[8,16,1024]{2,1,0:T(8,128)(2,1)} %shard_map.82), calls=%async_computation.2 | async-start | bytes 524288 | tf_op jit(solution)/shard_map/all_to_all | solution.py:279
